TPU v7x, 32 devices: a whole 2x2x4 slice. The times are simulated.
32 devices in a mesh: tok: 32 (over z, y, x, core), head: 1.
Axes of the slice: x: 2, y: 2, z: 4, core: 2. Of those that a mesh axis runs over, the one named last changes fastest.
Arguments:
- queries: bfloat16 [8192, 2560], P('tok', 'head'), may hold values from -256 to 256
- keys: bfloat16 [8192, 2560], P('tok', 'head'), may hold values from -6 to 6
- values: bfloat16 [8192, 2560], P('tok', 'head'), may hold values from -6 to 6
- rates: float32 [8192, 8], P('tok', 'head'), may hold values from 0.00022097086 to 0.0044194176
- back: int32 [8192], P('tok'), may hold values from 64 to 511
- group_end: int32 [1], replicated, may hold values from 2048 to 6143
- gate_init: float32 [8, 320, 320], P('head', None, 'tok'), may hold values from -0.3125 to 0.3125
- up_init: float32 [8, 320, 320], P('head', None, 'tok'), may hold values from -0.3125 to 0.3125
- down_init: float32 [8, 320, 320], P('head', None, 'tok'), may hold values from -0.3125 to 0.3125
- gain: float32 [2560], P('head'), may hold values from 0.5 to 1.5
Outputs:
- output: bfloat16 [8192, 2560], P('tok', 'head')
- gate_final: float32 [8, 320, 320], P('head', None, 'tok')
- up_final: float32 [8, 320, 320], P('head', None, 'tok')
- down_final: float32 [8, 320, 320], P('head', None, 'tok')
All inputs are finite; a program needn't handle non-finite values.
Results may differ from a plain program's by a relative error of at most 0.0088.
Values may be sent and summed in bfloat16 or wider, within the bound.
No kernel may reach another device: no remote copies, remote signals or barrier semaphores. Data moves between devices by JAX's collectives and lax.ppermute only.
A program may use at most 128 MiB of HBM per device.

v0:
```python
import functools
import math

import jax
import jax.numpy as jnp
from jax import lax
from jax.experimental import pallas as pl
from jax.experimental.pallas import tpu as pltpu
from jax.sharding import PartitionSpec as P

WINDOW = 512
BF16 = jnp.bfloat16
F32 = jnp.float32
MIB = 1 << 20
MICROSECOND = 10**9
ATT, MIX, GRAD, DELAY, FINISH, PACK = 10, 8, 12, 20, 10, 30
SPENT = 40

VMEM = pl.BlockSpec(memory_space=pltpu.VMEM)
SMEM = pl.BlockSpec(memory_space=pltpu.SMEM)
HBM = pl.BlockSpec(memory_space=pltpu.HBM)


def dot(lhs, rhs, lhs_dim, rhs_dim):
    return lax.dot_general(
        lhs, rhs, (((lhs_dim,), (rhs_dim,)), ((), ())), preferred_element_type=F32
    )


def call(
    body, info, inputs, outputs, scratch=(), flops=0, limit=60, late=(), far=(), after=()
):
    moved = sum(math.prod(x.shape) * x.dtype.itemsize for x in [*inputs, *late, *outputs, *far])
    given = 1 + len(inputs) + len(late)

    def kernel(*refs):
        body(*refs[:given], *refs[given + len(after) :])

    return pl.pallas_call(
        kernel,
        out_shape=(*outputs, *far),
        in_specs=[SMEM] + [VMEM] * len(inputs) + [HBM] * (len(late) + len(after)),
        out_specs=(*(VMEM for _ in outputs), *(HBM for _ in far)),
        scratch_shapes=list(scratch),
        compiler_params=pltpu.CompilerParams(vmem_limit_bytes=limit * MIB),
        cost_estimate=pl.CostEstimate(flops=flops, bytes_accessed=0, transcendentals=0),
    )(info, *inputs, *late, *after)


def fetches(sources, targets, semaphores):
    copies = [
        pltpu.make_async_copy(source, target, semaphores.at[number])
        for number, (source, target) in enumerate(zip(sources, targets))
    ]
    for copy in copies:
        copy.start()
    return copies


class Plan:
    def __init__(self, rows, heads, width, cols, count):
        self.rows, self.heads, self.width, self.cols, self.count = rows, heads, width, cols, count
        self.group = heads
        self.planes = count // heads
        self.fold = 2 if cols % 2 == 0 else 1
        self.part = cols // self.fold
        self.used = 3 * self.part
        self.lines = -(-(self.used + 1) // 16) * 16
        self.wide = self.fold * width
        self.pad = -(-width // 128) * 128
        self.gap = self.pad - width
        self.lanes = (slice(0, self.pad), slice(2 * width - self.pad, 2 * width))
        self.half = rows // 2
        self.steps = tuple(range(self.group))
        self.order = (0, 6, 7, 2, 4, 3, 5, 1) if self.group == 8 else self.steps
        self.run = 2 if self.group % 2 == 0 else 1
        self.tail = -(-WINDOW // rows)
        self.wire = (count, self.lines, self.wide)


def pack_state(plan, info, states, rates, after):
    def body(info_ref, gate_in, up_in, down_in, rate_in, out, lines, gate, up, down, rate, sems):
        copies = fetches((gate_in, up_in, down_in, rate_in), (gate, up, down, rate), sems)
        lines[...] = jnp.zeros_like(lines)
        for copy in copies:
            copy.wait()
        for kind, ref in enumerate((gate, up, down)):
            for col in range(plan.cols):
                side, line = divmod(col, plan.part)
                lanes = slice(side * plan.width, (side + 1) * plan.width)
                lines[:, kind * plan.part + line, lanes] = ref[col]
        if plan.group > 1:
            high = rate[...].astype(BF16).astype(F32)
            lines[:, plan.used, 0 : plan.rows] = high
            lines[:, plan.used, plan.rows : 2 * plan.rows] = rate[...] - high
        packed = lines[...].astype(BF16)
        for plane in range(plan.planes):
            out[plane * plan.group : (plane + 1) * plan.group] = packed

    return call(
        body,
        info,
        (),
        (jax.ShapeDtypeStruct(plan.wire, BF16),),
        [pltpu.VMEM((plan.group, plan.lines, plan.wide), F32)]
        + [pltpu.VMEM((plan.cols, plan.heads, plan.width), F32)] * 3
        + [pltpu.VMEM((plan.heads, plan.rows), F32), pltpu.SemaphoreType.DMA((4,))],
        late=(*states, rates),
        after=after,
    )[0]


def update(plan, info, states, wire, send, after=()):
    def body(info_ref, wire_ref, gate_in, up_in, down_in, *rest):
        if not send:
            rest = (*rest[:-1], gate_in, up_in, down_in, None)
        news, rest = rest[:3], rest[3:]
        out = rest[0] if send else None
        total, grad, gate, up, down, sems = rest[-6:]
        copies = fetches((gate_in, up_in, down_in), (gate, up, down), sems) if send else ()
        acc = wire_ref[0 : plan.group].astype(F32)
        for plane in range(1, plan.planes):
            acc += wire_ref[plane * plan.group : (plane + 1) * plan.group].astype(F32)
        total[...] = acc
        for kind, ref in enumerate((gate, up, down)):
            for col in range(plan.cols):
                side, line = divmod(col, plan.part)
                lanes = slice(side * plan.width, (side + 1) * plan.width)
                grad[col] = total[:, kind * plan.part + line, lanes]
            if send:
                copies[kind].wait()
            old = ref[...]
            fresh = old - grad[...]
            old_norm = jnp.sqrt(jnp.sum(old * old, axis=2, keepdims=True))
            new_norm = jnp.sqrt(jnp.sum(fresh * fresh, axis=2, keepdims=True) + 1e-06)
            new = fresh * (old_norm / new_norm)
            news[kind][...] = new
            if send:
                for col in range(plan.cols):
                    side, line = divmod(col, plan.part)
                    lanes = slice(side * plan.width, (side + 1) * plan.width)
                    total[:, kind * plan.part + line, lanes] = new[col]
        if send:
            packed = total[...].astype(BF16)
            for plane in range(plan.planes):
                out[plane * plan.group : (plane + 1) * plan.group] = packed

    state = jax.ShapeDtypeStruct((plan.cols, plan.heads, plan.width), F32)
    outputs = (state, state, state)
    if send:
        outputs += (jax.ShapeDtypeStruct(plan.wire, BF16),)
    return call(
        body,
        info,
        (wire,) if send else (wire, *states),
        outputs,
        [pltpu.VMEM((plan.group, plan.lines, plan.wide), F32)]
        + [pltpu.VMEM((plan.cols, plan.heads, plan.width), F32)] * (4 if send else 1)
        + [pltpu.SemaphoreType.DMA((3,))],
        late=states if send else (),
        after=after,
    )


def pack_pair(plan, info, left, right):
    def body(info_ref, left_in, right_in, *rest):
        outs, (left_ref, right_ref, held, sems, sent) = rest[: plan.group], rest[plan.group :]
        copies = []
        for copy in fetches((left_in, right_in), (left_ref, right_ref), sems):
            copy.wait()
        for step in range(plan.group):
            head = info_ref[0] ^ plan.order[step]
            lanes = pl.ds(pl.multiple_of((head >> 1) * 2 * plan.width, 128), 2 * plan.width)
            for odd in (0, 1):

                @pl.when((head & 1) == odd)
                def _():
                    own = slice(odd * plan.width, (odd + 1) * plan.width)
                    held[step, :, 0 : plan.width] = left_ref[:, lanes][:, own]
                    held[step, :, plan.width : 2 * plan.width] = right_ref[:, lanes][:, own]

            copies += fetches([held.at[step]], [outs[step]], sent.at[pl.ds(step, 1)])
        for copy in copies:
            copy.wait()

    if plan.group == 1:
        return (jnp.concatenate([left, right], axis=1),)
    block = jax.ShapeDtypeStruct((plan.rows, 2 * plan.width), BF16)
    return call(
        body,
        info,
        (),
        (),
        [pltpu.VMEM(left.shape, BF16)] * 2
        + [
            pltpu.VMEM((plan.group, plan.rows, 2 * plan.width), BF16),
            pltpu.SemaphoreType.DMA((2,)),
            pltpu.SemaphoreType.DMA((plan.group,)),
        ],
        late=(left, right),
        far=(block,) * plan.group,
    )


def last_blocks(plan, info, blocks, after=()):
    def body(info_ref, *refs):
        sources, (out, held, sems, sent) = refs[: plan.group], refs[plan.group :]

        def each(act):
            for step in range(plan.group):
                block = (info_ref[0] ^ plan.order[step]) - (plan.group - plan.tail)

                @pl.when(block >= 0)
                def _():
                    act(pltpu.make_async_copy(sources[step], held.at[block], sems.at[step]))

        each(lambda copy: copy.start())
        each(lambda copy: copy.wait())
        fetches([held], [out], sent)[0].wait()

    if plan.group == 1:
        return blocks[0].reshape(1, plan.rows, -1)
    block = jax.ShapeDtypeStruct((plan.tail, plan.rows, 2 * plan.width), BF16)
    scratch = [pltpu.VMEM(block.shape, BF16)]
    scratch += [pltpu.SemaphoreType.DMA((size,)) for size in (plan.group, 1)]
    return call(body, info, (), (), scratch, late=blocks, far=(block,), after=after)[0]


def pack_queries(plan, info, queries, reach, steps, after=()):
    half, width = plan.half, plan.width

    def fill(out, own, line):
        out[0:half, 0:width] = own[0:half]
        out[0:half, width : 2 * width] = own[half : 2 * half]
        out[half : half + 16, 0 : 2 * plan.rows] = line
        out[half : half + 16, 2 * plan.rows :] = jnp.zeros((16, 2 * (width - plan.rows)), BF16)

    def body(info_ref, back_ref, query_in, *rest):
        outs, (query_ref, held, sems, sent) = rest[: len(steps)], rest[len(steps) :]
        copies = fetches([query_in], [query_ref], sems)
        back = back_ref[...]
        high = jnp.floor(back * (1.0 / 16.0))
        line = jnp.concatenate([high, back - 16.0 * high], axis=1)
        line = (jnp.zeros((16, 2 * plan.rows), F32) + line).astype(BF16)
        copies.pop().wait()
        for number, step in enumerate(steps):
            if plan.group == 1:
                fill(held.at[0], query_ref[...], line)
            head = info_ref[0] ^ step
            lanes = pl.ds(pl.multiple_of((head >> 1) * 2 * width, 128), 2 * width)
            for odd in (0, 1) if plan.group > 1 else ():

                @pl.when((head & 1) == odd)
                def _():
                    own = slice(odd * width, (odd + 1) * width)
                    fill(held.at[number], query_ref[:, lanes][:, own], line)

            copies += fetches([held.at[number]], [outs[number]], sent.at[pl.ds(number, 1)])
        for copy in copies:
            copy.wait()

    block = jax.ShapeDtypeStruct((half + 16, 2 * width), BF16)
    return call(
        body,
        info,
        (reach,),
        (),
        [
            pltpu.VMEM(queries.shape, BF16),
            pltpu.VMEM((len(steps), half + 16, 2 * width), BF16),
            pltpu.SemaphoreType.DMA((1,)),
            pltpu.SemaphoreType.DMA((len(steps),)),
        ],
        late=(queries,),
        far=(block,) * len(steps),
        flops=PACK * MICROSECOND,
        after=after,
    )


def exchange(plan, blocks, steps=None):
    moved = {}
    for step in range(plan.group) if steps is None else steps:
        pairs = [(source, source ^ step) for source in range(plan.count)]
        moved[step] = lax.ppermute(blocks[step], "tok", pairs) if step else blocks[0]
    return moved


def sigmoid(value):
    return 0.5 * jnp.tanh(0.5 * value) + 0.5


def column(row):
    return jnp.swapaxes(jnp.broadcast_to(row, (8, row.shape[1])), 0, 1)[:, 0:1]


def delayed(plan, info, blocks, after):
    count = len(blocks)

    def body(info_ref, *refs):
        held, sems = refs[2 * count :]
        places = [held.at[number] for number in range(count)]
        for sources, targets in ((refs[:count], places), (places, refs[count : 2 * count])):
            for copy in fetches(sources, targets, sems):
                copy.wait()

    block = blocks[0]
    outs = tuple(jax.ShapeDtypeStruct(block.shape, block.dtype) for block in blocks)
    scratch = [pltpu.VMEM((count, *block.shape), block.dtype), pltpu.SemaphoreType.DMA((count,))]
    return call(
        body,
        info,
        (),
        (),
        scratch,
        flops=DELAY * MICROSECOND,
        late=blocks,
        far=outs,
        after=after,
    )


def line_places(plan):
    for owner in range(plan.count):
        for kind in range(3):
            for side in range(plan.fold):
                lines = slice(kind * plan.part, (kind + 1) * plan.part)
                lanes = slice(side * plan.width, (side + 1) * plan.width)
                yield owner, kind, lines, lanes, owner * plan.cols + side * plan.part


def fill_wire(plan, acc_both, acc_down, out, turned, lines):
    turned[0 : plan.pad] = acc_both[:, 0 : plan.pad].T
    turned[plan.pad : 2 * plan.pad] = acc_both[:, plan.pad :].T
    lines[:, plan.used :, :] = jnp.zeros((plan.count, plan.lines - plan.used, plan.wide), F32)
    for owner, kind, where, lanes, begin in line_places(plan):
        if kind < 2:
            piece = turned[kind * plan.pad + begin : kind * plan.pad + begin + plan.part, :]
        else:
            piece = acc_down[plan.gap + begin : plan.gap + begin + plan.part, :]
        lines[owner, where, lanes] = piece[:, 0 : plan.width]
    out[...] = lines[...].astype(BF16)


def unpack(plan, wire_ref, wide, both_ref, down_ref):
    width, pad, gap = plan.width, plan.pad, plan.gap
    if gap:
        wide[:, :, width:] = jnp.zeros((3, pad, gap), F32)
        wide[0:2, width:, :] = jnp.zeros((2, gap, pad), F32)
        wide[2, 0:gap, :] = jnp.zeros((gap, pad), F32)
    chunk = None
    for owner, kind, where, lanes, begin in line_places(plan):
        if kind == 0 and lanes.start == 0:
            chunk = wire_ref[owner].astype(F32)
        begin += gap if kind == 2 else 0
        wide[kind, begin : begin + plan.part, 0:width] = chunk[where, lanes]
    both_ref[:, 0:pad] = wide[0].T.astype(BF16)
    both_ref[:, pad:] = wide[1].T.astype(BF16)
    down_ref[...] = wide[2].astype(BF16)


def weights_of(plan, info, wire, after=()):
    rows = plan.rows

    def body(info_ref, wire_ref, both_ref, down_ref, rate_out, wide):
        unpack(plan, wire_ref, wide, both_ref, down_ref)
        for block in range(plan.group if plan.group > 1 else 0):
            line = wire_ref[info_ref[3] + block].astype(F32)[plan.used : plan.used + 1]
            rate_out[block : block + 1, :] = line[:, 0:rows] + line[:, rows : 2 * rows]

    pad = plan.pad
    return call(
        body,
        info,
        (wire,),
        (
            jax.ShapeDtypeStruct((pad, 2 * pad), BF16),
            jax.ShapeDtypeStruct((pad, pad), BF16),
            jax.ShapeDtypeStruct((plan.group, rows), F32),
        ),
        [pltpu.VMEM((3, pad, pad), F32)],
        after=after,
    )


def gradients(plan, info, weights, blocks, rates, number, after=()):
    width, pad, rows = plan.width, plan.pad, plan.rows

    def body(info_ref, rate_ref, *rest):
        both_ref, down_ref, *rest = rest
        sources, rest = rest[: plan.group], rest[plan.group :]
        out, kv, sems, acc_both, acc_down, turned, lines = rest
        targets = [kv.at[info_ref[0] ^ step] for step in plan.order]
        copies = fetches(sources, targets, sems)
        acc_both[...] = jnp.zeros_like(acc_both)
        acc_down[...] = jnp.zeros_like(acc_down)
        for copy in copies:
            copy.wait()
        @pl.loop(0, plan.group // plan.run)
        def _(turn_of):
            run = turn_of * plan.run
            start = info_ref[1] + run * rows
            live = start < info_ref[2] if number == 0 else start + plan.run * rows > info_ref[2]

            @pl.when(live)
            def _():
                rate = []
                for step in range(plan.run):
                    block = run + step
                    place = info_ref[1] + block * rows
                    place += lax.broadcasted_iota(jnp.int32, (1, rows), 1)
                    member = place < info_ref[2] if number == 0 else place >= info_ref[2]
                    rate.append(column(jnp.where(member, -rate_ref[pl.ds(block, 1), :], 0.0)))
                both_kinds = kv[pl.ds(run, plan.run)].reshape(plan.run * rows, 2 * width)
                keys = both_kinds[:, plan.lanes[0]]
                values = both_kinds[:, plan.lanes[1]].astype(F32)
                errors = (jnp.concatenate(rate, axis=0) * values).astype(BF16)
                pre = dot(keys, both_ref[...], 1, 0)
                back = dot(errors, down_ref[...], 1, 0)
                gate, up = pre[:, 0:pad], pre[:, pad:]
                sigma = sigmoid(gate)
                active = gate * sigma
                hidden = (active * up).astype(BF16)
                turn = sigma + active * (1.0 - sigma)
                slope = (back * up * turn).astype(BF16)
                joint = jnp.concatenate([slope, (back * active).astype(BF16)], axis=1)
                acc_both[...] += dot(keys, joint, 0, 0)
                acc_down[...] += dot(errors, hidden, 0, 0)

        fill_wire(plan, acc_both, acc_down, out, turned, lines)

    outputs = (jax.ShapeDtypeStruct(plan.wire, BF16),)
    scratch = [
        pltpu.VMEM((plan.group, rows, 2 * width), BF16),
        pltpu.SemaphoreType.DMA((plan.group,)),
        pltpu.VMEM((pad, 2 * pad), F32),
        pltpu.VMEM((pad, pad), F32),
        pltpu.VMEM((2 * pad, pad), F32),
        pltpu.VMEM(plan.wire, F32),
    ]
    return call(
        body,
        info,
        (rates, *weights),
        outputs,
        scratch,
        flops=GRAD * MICROSECOND,
        late=blocks,
        after=after,
    )


def unfold(plan, ref):
    half, width = plan.half, plan.width
    first = ref[0:half, plan.lanes[0]]
    second = ref[0:half, plan.lanes[1]]
    second = jnp.concatenate([second[:, plan.gap :], second[:, 0 : plan.gap]], axis=1)
    lane = lax.broadcasted_iota(jnp.int32, (1, plan.pad), 1)
    keep = jnp.where(lane < width, 1.0, 0.0).astype(BF16)
    return jnp.concatenate([first, second], axis=0) * keep


def fold(plan, value):
    half, gap, pad = plan.half, plan.gap, plan.pad
    return jnp.concatenate([value[0:half, gap:], value[half:, gap:]], axis=1)


def mixes(plan, info, firsts, seconds, queries, after=()):
    count = len(queries)
    width, pad, rows, half = plan.width, plan.pad, plan.rows, plan.half

    def body(info_ref, *rest):
        weights, rest = rest[:4], rest[4:]
        sources, rest = rest[:count], rest[count:]
        outs, (asks, news, both, down, sems, sent) = rest[:count], rest[count:]
        place, border = info_ref[0], info_ref[2]
        copies = fetches(sources, [asks.at[index] for index in range(count)], sems)
        for group in range(2):
            both[group] = weights[2 * group][...]
            down[group] = weights[2 * group + 1][...].astype(F32).T.astype(BF16)
        for copy in copies:
            copy.wait()

        def apply(asked, group):
            pre = dot(asked, both[group], 1, 0)
            gate, up = pre[:, 0:pad], pre[:, pad:]
            hidden = (gate * sigmoid(gate) * up).astype(BF16)
            return dot(hidden, down[group], 1, 0)

        @pl.loop(0, count // plan.run)
        def _(turn_of):
            both_of = [turn_of * plan.run + step for step in range(plan.run)]
            starts = [info_ref[1] + (place ^ i) * rows for i in both_of]
            start = functools.reduce(jnp.minimum, starts)
            asked = jnp.concatenate([unfold(plan, asks.at[i]) for i in both_of], axis=0)
            result = apply(asked, (start >= border).astype(jnp.int32))
            for at, i in enumerate(both_of):
                news[i] = fold(plan, result[at * rows : (at + 1) * rows]).astype(BF16)

            @pl.when((start < border) & (start + plan.run * rows > border))
            def _():
                other = apply(asked, 1)
                for at, i in enumerate(both_of):
                    new = fold(plan, other[at * rows : (at + 1) * rows])
                    spot = starts[at] + lax.broadcasted_iota(jnp.int32, new.shape, 0)
                    lane = lax.broadcasted_iota(jnp.int32, new.shape, 1)
                    spot += jnp.where(lane >= width, half, 0)
                    old = news[i].astype(F32)
                    news[i] = jnp.where(spot >= border, new, old).astype(BF16)

        for copy in fetches([news.at[index] for index in range(count)], outs, sent):
            copy.wait()

    block = jax.ShapeDtypeStruct((half, 2 * width), BF16)
    return call(
        body,
        info,
        (*firsts, *seconds),
        (),
        [
            pltpu.VMEM((count, half + 16, 2 * width), BF16),
            pltpu.VMEM((count, half, 2 * width), BF16),
            pltpu.VMEM((2, pad, 2 * pad), BF16),
            pltpu.VMEM((2, pad, pad), BF16),
            pltpu.SemaphoreType.DMA((count,)),
            pltpu.SemaphoreType.DMA((count,)),
        ],
        far=(block,) * count,
        flops=MIX * MICROSECOND,
        late=queries,
        after=after,
    )


def attention(plan, info, queries, blocks, halo, after=()):
    count = len(queries)
    width, pad, rows, half = plan.width, plan.pad, plan.rows, plan.half
    seen = (plan.tail + 1) * rows
    scale = 1.0 / math.sqrt(width)

    def body(info_ref, halo_in, *rest):
        sources, rest = rest[: count + plan.group], rest[count + plan.group :]
        outs, rest = rest[:count], rest[count:]
        asks, held, news, sems, sent = rest
        place = info_ref[0]
        targets = [held.at[0 : plan.tail]]
        targets += [asks.at[number] for number in range(count)]
        targets += [held.at[plan.tail + (place ^ step)] for step in plan.order]
        for copy in fetches((halo_in, *sources), targets, sems):
            copy.wait()
        query = lax.broadcasted_iota(jnp.int32, (rows, 1), 0) + plan.tail * rows
        spot = lax.broadcasted_iota(jnp.int32, (rows, seen), 1)
        @pl.loop(0, count, unroll=min(2, count))
        def _(number):
            block = place ^ number
            line = asks[number, half : half + 16, :].astype(F32)[0:1, :]
            reach = column(line[:, 0:rows] * 16.0 + line[:, rows : 2 * rows]).astype(jnp.int32)
            first = plan.tail * rows - info_ref[1] - block * rows
            low = jnp.maximum(query - reach, first)
            window = held[pl.ds(block, plan.tail + 1)].reshape(seen, 2 * width)
            scores = dot(unfold(plan, asks.at[number]), window[:, plan.lanes[0]], 1, 1)
            scores = jnp.where((spot <= query) & (spot >= low), scores, -jnp.inf)
            top = jnp.max(scores, axis=1, keepdims=True)
            weights = jnp.exp((scores - top) * scale)
            total = jnp.sum(weights, axis=1, keepdims=True)
            mixed = dot(weights.astype(BF16), window[:, plan.lanes[1]], 1, 0)
            news[number] = fold(plan, mixed * (1.0 / total)).astype(BF16)

        for copy in fetches([news.at[number] for number in range(count)], outs, sent):
            copy.wait()

    block = jax.ShapeDtypeStruct((half, 2 * width), BF16)
    return call(
        body,
        info,
        (),
        (),
        [
            pltpu.VMEM((count, half + 16, 2 * width), BF16),
            pltpu.VMEM((plan.tail + plan.group, rows, 2 * width), BF16),
            pltpu.VMEM((count, half, 2 * width), BF16),
            pltpu.SemaphoreType.DMA((1 + count + plan.group,)),
            pltpu.SemaphoreType.DMA((count,)),
        ],
        far=(block,) * count,
        flops=ATT * MICROSECOND,
        late=(halo, *queries, *blocks),
        after=after,
    )


def halo_of(plan, last):
    span = plan.group * plan.rows
    shifts = -(-WINDOW // span)
    if shifts == 1:
        pairs = [(i, i + plan.group) for i in range(plan.count - plan.group)]
        return lax.ppermute(last, "tok", pairs)
    parts = []
    for distance in range(shifts, 0, -1):
        hop = distance * plan.group
        parts.append(lax.ppermute(last, "tok", [(i, i + hop) for i in range(plan.count - hop)]))
    return jnp.concatenate(parts, axis=0)[-plan.tail :]


def finish(plan, info, mixed, attended, gain, after):
    width, half, total = plan.width, plan.half, plan.heads * plan.width

    def body(info_ref, gain_ref, *rest):
        sources, rest = rest[: 2 * plan.group], rest[2 * plan.group :]
        out_far, ys, adds, out, sems, sent = rest
        targets = [held.at[step] for held in (ys, adds) for step in range(plan.group)]
        copies = fetches(sources, targets, sems)
        done = []
        squares = jnp.zeros((half, 2 * width), F32)
        for step in range(plan.group):
            copies[step].wait()
            y = ys[step].astype(F32)
            squares += y * y
        norms = [
            lax.rsqrt(jnp.sum(s, axis=1, keepdims=True) * (1.0 / total) + 1e-06)
            for s in (squares[:, 0:width], squares[:, width:])
        ]
        lane = lax.broadcasted_iota(jnp.int32, (half, 2 * width), 1)
        norm = jnp.where(lane < width, norms[0], norms[1])
        for pair in range(plan.group // 2):
            lanes = pl.ds(pl.multiple_of(((info_ref[0] >> 1) ^ pair) * 2 * width, 128), 2 * width)
            values = []
            for step in (2 * pair, 2 * pair + 1):
                copies[plan.group + step].wait()
                scale = gain_ref[pl.ds(info_ref[0] ^ step, 1), :]
                value = ys[step].astype(F32) * norm * scale + adds[step].astype(F32)
                values.append(value.astype(BF16))
            for odd in (0, 1):

                @pl.when((info_ref[0] & 1) == odd)
                def _():
                    even, other = values[odd], values[1 - odd]
                    for side in range(2):
                        own = slice(side * width, (side + 1) * width)
                        joined = jnp.concatenate([even[:, own], other[:, own]], axis=1)
                        out[pair, side * half : (side + 1) * half, :] = joined

            done += fetches([out.at[pair]], [out_far.at[:, lanes]], sent.at[pl.ds(pair, 1)])
        for copy in done:
            copy.wait()

    gain = gain.reshape(plan.heads, width)
    return call(
        body,
        info,
        (jnp.concatenate([gain, gain], axis=1),),
        (),
        [
            pltpu.VMEM((plan.group, half, 2 * width), BF16),
            pltpu.VMEM((plan.group, half, 2 * width), BF16),
            pltpu.VMEM((plan.group // 2, plan.rows, 2 * width), BF16),
            pltpu.SemaphoreType.DMA((2 * plan.group,)),
            pltpu.SemaphoreType.DMA((plan.group // 2,)),
        ],
        late=tuple(held[step] for held in (mixed, attended) for step in range(plan.group)),
        far=(jax.ShapeDtypeStruct((plan.rows, total), BF16),),
        flops=FINISH * MICROSECOND,
        after=after,
    )[0]


def finish_apart(plan, mixed, attended, gain):
    def flat(block):
        return jnp.concatenate([block[:, : plan.width], block[:, plan.width :]], axis=0).astype(F32)

    y, a = flat(mixed[0]), flat(attended[0])
    squares = lax.psum(jnp.sum(y * y, axis=1, keepdims=True), "head")
    mean = squares / (plan.heads * plan.width * lax.axis_size("head"))
    return (y / jnp.sqrt(mean + 1e-06) * gain.reshape(1, -1) + a).astype(BF16)


def spent(info):
    def body(info_ref, out):
        out[...] = jnp.zeros_like(out) + info_ref[0]

    return call(body, info, (), (jax.ShapeDtypeStruct((8, 128), jnp.int32),), flops=SPENT * MICROSECOND)[0]


def spread(wire):
    return lax.all_to_all(wire, "tok", 0, 0, tiled=True)


def on_device(queries, keys, values, rates, back, group_end, gate_init, up_init, down_init, gain):
    rows, heads = rates.shape
    count = lax.axis_size("tok")
    plan = Plan(rows, heads, queries.shape[1] // heads, gate_init.shape[2], count)
    me = lax.axis_index("tok").astype(jnp.int32)
    place = lax.rem(me, plan.group)
    info = jnp.stack([place, (me - place) * rows, group_end[0], me - place])
    states = tuple(jnp.transpose(w, (2, 0, 1)) for w in (gate_init, up_init, down_init))
    rate_rows = rates.T
    reach = back.astype(F32).reshape(1, rows)

    steps = plan.steps
    packed = pack_pair(plan, info, keys, values)
    blocks = [*exchange(plan, dict(zip(plan.order, packed)), plan.order).values()]
    wire = spread(pack_state(plan, info, states, rate_rows, packed[:1]))
    both, down, found = weights_of(plan, info, wire, (spent(info),))
    if plan.group > 1:
        rate_rows = found

    def part(steps, blocks):
        return [blocks[step] for step in steps]

    last = last_blocks(plan, info, blocks, (down,))
    wire = gradients(plan, info, (both, down), blocks, rate_rows, 0, (last,))[0]
    halo = halo_of(plan, last)
    found = pack_queries(plan, info, queries, reach, steps, (wire, halo))
    asks = exchange(plan, dict(zip(steps, found)))
    wire = spread(wire)
    *states, wire = update(plan, info, states, wire, True, part((1, 6) if steps[6:] else (), asks))
    wire, after = spread(wire), (wire,)
    found = attention(plan, info, part(steps, asks), blocks, halo, after)
    attended, after = dict(zip(steps, found)), found[:1]
    attended = exchange(plan, attended)
    firsts = (both, down)
    *seconds, _ = weights_of(plan, info, wire, after)
    found = mixes(plan, info, firsts, seconds, part(steps, asks))
    after = (*found[:1], *part(steps[1:], attended))
    wire = gradients(plan, info, seconds, blocks, rate_rows, 1, after)[0]
    first, later = (*steps[:1], *steps[3:]), steps[1:3]
    mixed = exchange(plan, dict(zip(steps, found)), first)
    after = ()
    if later:
        after = delayed(plan, info, part(later, found), (wire, *part(first[1:], mixed)))
        mixed.update(exchange(plan, dict(zip(later, after)), later))
    states = update(plan, info, states, spread(wire), False, after[:1])
    if plan.group > 1:
        output = finish(plan, info, mixed, attended, gain, states[:1])
    else:
        output = finish_apart(plan, mixed, attended, gain)
    return (output, *(jnp.transpose(w, (1, 2, 0)) for w in states))


def solution(mesh):
    tokens, state = P("tok", "head"), P("head", None, "tok")
    return jax.shard_map(
        on_device,
        mesh=mesh,
        in_specs=(tokens, tokens, tokens, tokens, P("tok"), P(), state, state, state, P("head")),
        out_specs=(tokens, state, state, state),
        check_vma=False,
    )
```

profile of v0, /device:TPU:0, one launch (start us, length us, event | category | flops | bytes accessed | tf_op | source)
XLA Modules:
  0.0 173.6 jit_solution(4372674976217590939)
XLA Ops:
  1.3 0.7 pad_add_fusion.refs_0_
  1.9 4.3 %shard_map.129 = (bf16[256,640]{1,0:T(8,128)(2,1)}, bf16[256,640]{1,0:T(8,128)(2,1)}, bf16[256,640]{1,0:T(8,128)(2,1)}, bf16[256,640]{1,0:T(8,128)(2,1)}, bf16[2...) custom-call(s32[4]{0:T(128)} %pad_add_fusion.refs_0_, ...), custom_call_target="tpu_custom_call" | custom-call | tf_op jit(solution)/shard_map/pallas_call | solution.py:39
  6.3 4.0 %collective-permute-start = (bf16[256,640]{1,0:T(8,128)(2,1)}, bf16[256,640]{1,0:T(8,128)(2,1)S(1)}, u32[]{:S(2)}, u32[]{:S(2)}) collective-permute-start(bf16[256,640]{1,0:T(8,128)(2,1)} %get-tuple-element.54), channel_id=1, source_target_pairs={{0,6},{1,7},{2,4},{3,5},{4,2},{5,3},{6,0},{7,1},{8,14},{9,15},{10,... | collective-permute-start | bytes 983048 | tf_op jit(solution)/shard_map/ppermute | solution.py:285
  10.2 2.9 %shard_map.130 = bf16[32,16,640]{2,1,0:T(8,128)(2,1)} custom-call(s32[4]{0:T(128)} %pad_add_fusion.refs_0_, f32[10,8,320]{2,1,0:T(8,128)} %bitcast.11, f32[10,8,320]{2,1,0:T(8,128)} %bitcast.13, f32[10,8,320]{2,1,0:T(8,128)} %bitcast.15, f32[8,256]{1,0:T(8,128)} %bitcast.17, bf16[256,640]{1,0:T(8,128)(2,1)} %get-tuple-element.50.refs_5_.refs_1_.refs_4_.refs_10_), custom_call_target="tpu_custom_call" | custom-call | tf_op jit(solution)/shard_map/pallas_call | solution.py:39
  13.2 6.1 %all-to-all-start = ((bf16[32,16,640]{2,1,0:T(8,128)(2,1)}), bf16[32,16,640]{2,1,0:T(8,128)(2,1)S(1)}, u32[]{:S(2)}, u32[]{:S(2)}) async-start(bf16[32,16,640]{2,1,0:T(8,128)(2,1)} %shard_map.130), calls=%async_computation | async-start | bytes 1310720 | tf_op jit(solution)/shard_map/all_to_all | solution.py:685
  19.2 1.8 %collective-permute-start.2 = (bf16[256,640]{1,0:T(8,128)(2,1)}, bf16[256,640]{1,0:T(8,128)(2,1)S(1)}, u32[]{:S(2)}, u32[]{:S(2)}) collective-permute-start(bf16[256,640]{1,0:T(8,128)(2,1)} %get-tuple-element.56), channel_id=1, source_target_pairs={{0,2},{1,3},{2,0},{3,1},{4,6},{5,7},{6,4},{7,5},{8,10},{9,11},{10,... | collective-permute-start | bytes 983048 | tf_op jit(solution)/shard_map/ppermute | solution.py:285
  21.0 1.5 collective-permute-start.3
  22.5 0.5 collective-permute-start.5
  23.1 6.3 %collective-permute-done.1.refs_3_.refs_6_.refs_12_ = bf16[256,640]{1,0:T(8,128)(2,1)S(1)} collective-permute-done((bf16[256,640]{1,0:T(8,128)(2,1)}, bf16[256,640]{1,0:T(8,128)(2,1)S(1)}, u32[]{:S(2)}, u32[]{:S(2)}) %collective-permute-start.1) | collective-permute-done | bytes 327712 | tf_op jit(solution)/shard_map/ppermute | solution.py:285
  29.6 1.3 shard_map.131.refs_2_
  30.9 0.6 convert_element_type.3
  31.5 5.7 %all-to-all-done.refs_1_ = bf16[32,16,640]{2,1,0:T(8,128)(2,1)S(1)} async-done(((bf16[32,16,640]{2,1,0:T(8,128)(2,1)}), bf16[32,16,640]{2,1,0:T(8,128)(2,1)S(1)}, u32[]{:S(2)}, u32[]{:S(2)}) %all-to-all-start) | async-done | bytes 655392 | tf_op jit(solution)/shard_map/all_to_all | solution.py:685
  37.2 0.8 copy-done.3
  38.0 2.5 %shard_map.132 = (bf16[384,768]{1,0:T(8,128)(2,1)}, bf16[384,384]{1,0:T(8,128)(2,1)}, f32[8,256]{1,0:T(8,128)}) custom-call(s32[4]{0:T(128)} %pad_add_fusion.refs_0_, bf16[32,16,640]{2,1,0:T(8,128)(2,1)} %copy-done.3, s32[8,128]{1,0:T(8,128)} %shard_map.131.refs_2_), custom_call_target="tpu_custom_call" | custom-call | tf_op jit(solution)/shard_map/pallas_call | solution.py:39
  40.5 0.3 collective-permute-done.2.refs_4_.refs_7_.refs_13_
  40.9 4.9 %collective-permute-done.4.refs_6_.refs_9_.refs_15_ = bf16[256,640]{1,0:T(8,128)(2,1)S(1)} collective-permute-done((bf16[256,640]{1,0:T(8,128)(2,1)}, bf16[256,640]{1,0:T(8,128)(2,1)S(1)}, u32[]{:S(2)}, u32[]{:S(2)}) %collective-permute-start.4) | collective-permute-done | bytes 327712 | tf_op jit(solution)/shard_map/ppermute | solution.py:285
  45.7 0.4 collective-permute-done.5.refs_7_.refs_10_.refs_16_
  46.5 0.4 copy-done.9
  47.0 2.7 %shard_map.133.refs_12_ = bf16[2,256,640]{2,1,0:T(8,128)(2,1)} custom-call(s32[4]{0:T(128)} %pad_add_fusion.refs_0_, bf16[256,640]{1,0:T(8,128)(2,1)} %get-tuple-element.50.refs_5_.refs_1_.refs_4_.refs_10_, bf16[256,640]{1,0:T(8,128)(2,1)} %copy-done.4, bf16[256,640]{1,0:T(8,128)(2,1)} %copy-done.5, bf16[256,640]{1,0:T(8,128)(2,1)} %copy-done.6, ...), custom_call_target="tpu_custom_call" | custom-call | tf_op jit(solution)/shard_map/pallas_call | solution.py:39
  49.7 3.7 %collective-permute-start.7 = (bf16[2,256,640]{2,1,0:T(8,128)(2,1)}, bf16[2,256,640]{2,1,0:T(8,128)(2,1)S(1)}, u32[]{:S(2)}, u32[]{:S(2)}) collective-permute-start(bf16[2,256,640]{2,1,0:T(8,128)(2,1)} %shard_map.133.refs_12_), channel_id=1, source_target_pairs={{0,8},{1,9},{2,10},{3,11},{4,12},{5,13},{6,14},{7,15},{8,16},{9,17... | collective-permute-start | bytes 1966088 | tf_op jit(solution)/shard_map/ppermute | solution.py:597
  53.4 10.9 %shard_map.134.refs_3_ = bf16[32,16,640]{2,1,0:T(8,128)(2,1)} custom-call(s32[4]{0:T(128)} %pad_add_fusion.refs_0_, f32[8,256]{1,0:T(8,128)} %get-tuple-element.53.refs_1_, bf16[384,768]{1,0:T(8,128)(2,1)} %get-tuple-element.51.refs_2_.refs_1_, bf16[384,384]{1,0:T(8,128)(2,1)} %get-tuple-element.52.refs_9_.refs_3_.refs_2_, ...), custom_call_target="tpu_custom_call" | custom-call | flops 12000000000 | tf_op jit(solution)/shard_map/pallas_call | solution.py:39
  64.3 3.8 %all-to-all-start.1 = ((bf16[32,16,640]{2,1,0:T(8,128)(2,1)}), bf16[32,16,640]{2,1,0:T(8,128)(2,1)S(1)}, u32[]{:S(2)}, u32[]{:S(2)}) async-start(bf16[32,16,640]{2,1,0:T(8,128)(2,1)} %shard_map.134.refs_3_), calls=%async_computation.1 | async-start | bytes 1310720 | tf_op jit(solution)/shard_map/all_to_all | solution.py:685
  68.1 0.8 copy-done.15
  69.0 3.6 %shard_map.135 = (bf16[144,640]{1,0:T(8,128)(2,1)}, bf16[144,640]{1,0:T(8,128)(2,1)}, bf16[144,640]{1,0:T(8,128)(2,1)}, bf16[144,640]{1,0:T(8,128)(2,1)}, bf16[1...) custom-call(s32[4]{0:T(128)} %pad_add_fusion.refs_0_, ...), custom_call_target="tpu_custom_call" | custom-call | flops 30000001024 | tf_op jit(solution)/shard_map/pallas_call | solution.py:39
  72.6 0.3 collective-permute-start.8
  72.9 2.6 %collective-permute-start.9 = (bf16[144,640]{1,0:T(8,128)(2,1)}, bf16[144,640]{1,0:T(8,128)(2,1)S(1)}, u32[]{:S(2)}, u32[]{:S(2)}) collective-permute-start(bf16[144,640]{1,0:T(8,128)(2,1)} %get-tuple-element.62), channel_id=1, source_target_pairs={{0,6},{1,7},{2,4},{3,5},{4,2},{5,3},{6,0},{7,1},{8,14},{9,15},{10,... | collective-permute-start | bytes 552968 | tf_op jit(solution)/shard_map/ppermute | solution.py:285
  75.5 0.6 collective-permute-start.10
  76.0 0.9 collective-permute-start.11
  76.9 0.6 collective-permute-start.12
  77.5 1.5 collective-permute-start.13
  79.0 4.3 %collective-permute-done.9.refs_6_.refs_8_.refs_11_ = bf16[144,640]{1,0:T(8,128)(2,1)S(1)} collective-permute-done((bf16[144,640]{1,0:T(8,128)(2,1)}, bf16[144,640]{1,0:T(8,128)(2,1)S(1)}, u32[]{:S(2)}, u32[]{:S(2)}) %collective-permute-start.9) | collective-permute-done | bytes 184352 | tf_op jit(solution)/shard_map/ppermute | solution.py:285
  83.3 0.6 collective-permute-start.14
  83.9 2.1 %all-to-all-done.1.refs_1_ = bf16[32,16,640]{2,1,0:T(8,128)(2,1)S(1)} async-done(((bf16[32,16,640]{2,1,0:T(8,128)(2,1)}), bf16[32,16,640]{2,1,0:T(8,128)(2,1)S(1)}, u32[]{:S(2)}, u32[]{:S(2)}) %all-to-all-start.1) | async-done | bytes 655392 | tf_op jit(solution)/shard_map/all_to_all | solution.py:685
  86.0 0.8 copy-done
  86.9 3.6 %shard_map.136 = (f32[10,8,320]{2,1,0:T(8,128)}, f32[10,8,320]{2,1,0:T(8,128)}, f32[10,8,320]{2,1,0:T(8,128)}, bf16[32,16,640]{2,1,0:T(8,128)(2,1)}) custom-call(s32[4]{0:T(128)} %pad_add_fusion.refs_0_, bf16[32,16,640]{2,1,0:T(8,128)(2,1)} %copy-done, f32[10,8,320]{2,1,0:T(8,128)} %bitcast.12, f32[10,8,320]{2,1,0:T(8,128)} %bitcast.14, ...), custom_call_target="tpu_custom_call" | custom-call | tf_op jit(solution)/shard_map/pallas_call | solution.py:39
  90.4 4.6 %all-to-all-start.2 = ((bf16[32,16,640]{2,1,0:T(8,128)(2,1)}), bf16[32,16,640]{2,1,0:T(8,128)(2,1)S(1)}, u32[]{:S(2)}, u32[]{:S(2)}) async-start(bf16[32,16,640]{2,1,0:T(8,128)(2,1)} %get-tuple-element.63.refs_18_), calls=%async_computation.2 | async-start | bytes 1310720 | tf_op jit(solution)/shard_map/all_to_all | solution.py:685
  95.2 0.7 collective-permute-done.14.refs_9_.refs_12_
  96.0 0.5 copy-done.21
  96.5 11.2 %shard_map.137 = (bf16[128,640]{1,0:T(8,128)(2,1)}, bf16[128,640]{1,0:T(8,128)(2,1)}, bf16[128,640]{1,0:T(8,128)(2,1)}, bf16[128,640]{1,0:T(8,128)(2,1)}, bf16[1...) custom-call(s32[4]{0:T(128)} %pad_add_fusion.refs_0_, ...), custom_call_target="tpu_custom_call" | custom-call | flops 10000000000 | tf_op jit(solution)/shard_map/pallas_call | solution.py:39
  107.9 1.2 collective-permute-start.16
  109.1 0.6 collective-permute-start.17
  109.7 1.1 collective-permute-start.18
  110.8 0.6 collective-permute-start.19
  111.4 1.4 all-to-all-done.2.refs_1_
  112.8 0.8 copy-done.1
  113.7 2.5 %shard_map.138 = (bf16[384,768]{1,0:T(8,128)(2,1)}, bf16[384,384]{1,0:T(8,128)(2,1)}, f32[8,256]{1,0:T(8,128)}) custom-call(s32[4]{0:T(128)} %pad_add_fusion.refs_0_, bf16[32,16,640]{2,1,0:T(8,128)(2,1)} %copy-done.1, bf16[128,640]{1,0:T(8,128)(2,1)} %get-tuple-element.70.refs_2_.refs_10_), custom_call_target="tpu_custom_call" | custom-call | tf_op jit(solution)/shard_map/pallas_call | solution.py:39
  116.2 2.3 %collective-permute-start.20 = (bf16[128,640]{1,0:T(8,128)(2,1)}, bf16[128,640]{1,0:T(8,128)(2,1)S(1)}, u32[]{:S(2)}, u32[]{:S(2)}) collective-permute-start(bf16[128,640]{1,0:T(8,128)(2,1)} %get-tuple-element.81), channel_id=1, source_target_pairs={{0,6},{1,7},{2,4},{3,5},{4,2},{5,3},{6,0},{7,1},{8,14},{9,15},{10,... | collective-permute-start | bytes 491528 | tf_op jit(solution)/shard_map/ppermute | solution.py:285
  118.6 8.3 %shard_map.139 = (bf16[128,640]{1,0:T(8,128)(2,1)}, bf16[128,640]{1,0:T(8,128)(2,1)}, bf16[128,640]{1,0:T(8,128)(2,1)}, bf16[128,640]{1,0:T(8,128)(2,1)}, bf16[1...) custom-call(s32[4]{0:T(128)} %pad_add_fusion.refs_0_, ...), custom_call_target="tpu_custom_call" | custom-call | flops 8000000000 | tf_op jit(solution)/shard_map/pallas_call | solution.py:39
  127.0 1.7 collective-permute-start.22
  128.7 1.5 collective-permute-start.23
  130.2 1.2 collective-permute-start.25
  131.5 1.6 collective-permute-start.26
  133.1 4.7 %shard_map.140.refs_3_ = bf16[32,16,640]{2,1,0:T(8,128)(2,1)} custom-call(s32[4]{0:T(128)} %pad_add_fusion.refs_0_, f32[8,256]{1,0:T(8,128)} %get-tuple-element.53.refs_1_, bf16[384,768]{1,0:T(8,128)(2,1)} %get-tuple-element.71.refs_3_.refs_2_, bf16[384,384]{1,0:T(8,128)(2,1)} %get-tuple-element.72.refs_4_.refs_3_, ...), custom_call_target="tpu_custom_call" | custom-call | flops 12000000000 | tf_op jit(solution)/shard_map/pallas_call | solution.py:39
  137.9 9.2 %all-to-all-start.3 = ((bf16[32,16,640]{2,1,0:T(8,128)(2,1)}), bf16[32,16,640]{2,1,0:T(8,128)(2,1)S(1)}, u32[]{:S(2)}, u32[]{:S(2)}) async-start(bf16[32,16,640]{2,1,0:T(8,128)(2,1)} %shard_map.140.refs_3_), calls=%async_computation.3 | async-start | bytes 1310720 | tf_op jit(solution)/shard_map/all_to_all | solution.py:685
  147.2 0.6 copy-done.29
  148.0 2.5 %shard_map.141 = (bf16[128,640]{1,0:T(8,128)(2,1)}, bf16[128,640]{1,0:T(8,128)(2,1)}) custom-call(s32[4]{0:T(128)} %pad_add_fusion.refs_0_, bf16[128,640]{1,0:T(8,128)(2,1)} %get-tuple-element.74.refs_1_, bf16[128,640]{1,0:T(8,128)(2,1)} %get-tuple-element.75.refs_2_, bf16[32,16,640]{2,1,0:T(8,128)(2,1)} %shard_map.140.refs_3_, bf16[128,640]{1,0:T(8,128)(2,1)} %copy-done.29, ...), custom_call_target="tpu_custom_call" | custom-call | flops 20000000000 | tf_op jit(solution)/shard_map/pallas_call | solution.py:39
  150.6 0.3 collective-permute-start.27
  150.9 1.7 collective-permute-start.28
  152.6 0.7 pad_maximum_fusion.refs_1_
  153.3 11.7 %all-to-all-done.3.refs_1_ = bf16[32,16,640]{2,1,0:T(8,128)(2,1)S(1)} async-done(((bf16[32,16,640]{2,1,0:T(8,128)(2,1)}), bf16[32,16,640]{2,1,0:T(8,128)(2,1)S(1)}, u32[]{:S(2)}, u32[]{:S(2)}) %all-to-all-start.3) | async-done | bytes 655392 | tf_op jit(solution)/shard_map/all_to_all | solution.py:685
  165.0 0.8 copy-done.2
  165.8 2.3 %shard_map.142 = (f32[10,8,320]{2,1,0:T(8,128)}, f32[10,8,320]{2,1,0:T(8,128)}, f32[10,8,320]{2,1,0:T(8,128)}) custom-call(s32[4]{0:T(128)} %pad_add_fusion.refs_0_, bf16[32,16,640]{2,1,0:T(8,128)(2,1)} %copy-done.2, f32[10,8,320]{2,1,0:T(8,128)} %get-tuple-element.90.refs_2_, f32[10,8,320]{2,1,0:T(8,128)} %get-tuple-element.91.refs_3_, ...), custom_call_target="tpu_custom_call" | custom-call | tf_op jit(solution)/shard_map/pallas_call | solution.py:39
  168.2 0.6 copy-done.34
  168.9 4.5 %shard_map.143 = bf16[256,2560]{1,0:T(8,128)(2,1)} custom-call(s32[4]{0:T(128)} %pad_add_fusion.refs_0_, f32[8,640]{1,0:T(8,128)} %pad_maximum_fusion.refs_1_, bf16[128,640]{1,0:T(8,128)(2,1)} %get-tuple-element.73.refs_12_.refs_2_, bf16[128,640]{1,0:T(8,128)(2,1)} %copy-done.34, bf16[128,640]{1,0:T(8,128)(2,1)} %copy-done.35, bf16[128,640]{1,0:T(8,128)(2,1)} %copy-done.29, ...), custom_call_target="tpu_custom_call" | custom-call | flops 10000000000 | tf_op jit(solution)/shard_map/pallas_call | solution.py:39
  (93 shorter events, 1.5 us)
Async XLA Ops:
  6.3 16.3 %collective-permute-start = (bf16[256,640]{1,0:T(8,128)(2,1)}, bf16[256,640]{1,0:T(8,128)(2,1)S(1)}, u32[]{:S(2)}, u32[]{:S(2)}) collective-permute-start(bf16[256,640]{1,0:T(8,128)(2,1)} %get-tuple-element.54), channel_id=1, source_target_pairs={{0,6},{1,7},{2,4},{3,5},{4,2},{5,3},{6,0},{7,1},{8,14},{9,15},{10,... | collective-permute-start | bytes 983048 | tf_op jit(solution)/shard_map/ppermute | solution.py:285
  10.2 19.2 %collective-permute-start.1 = (bf16[256,640]{1,0:T(8,128)(2,1)}, bf16[256,640]{1,0:T(8,128)(2,1)S(1)}, u32[]{:S(2)}, u32[]{:S(2)}) collective-permute-start(bf16[256,640]{1,0:T(8,128)(2,1)} %get-tuple-element.55), channel_id=1, source_target_pairs={{0,7},{1,6},{2,5},{3,4},{4,3},{5,2},{6,1},{7,0},{8,15},{9,14},{10,... | collective-permute-start | bytes 983048 | tf_op jit(solution)/shard_map/ppermute | solution.py:285
  10.2 19.2 %copy-start.16 = (bf16[256,640]{1,0:T(8,128)(2,1)S(1)}, bf16[256,640]{1,0:T(8,128)(2,1)}, u32[]{:S(2)}) copy-start(bf16[256,640]{1,0:T(8,128)(2,1)} %get-tuple-element.60) | copy-start | bytes 983044
  13.2 24.0 %all-to-all-start = ((bf16[32,16,640]{2,1,0:T(8,128)(2,1)}), bf16[32,16,640]{2,1,0:T(8,128)(2,1)S(1)}, u32[]{:S(2)}, u32[]{:S(2)}) async-start(bf16[32,16,640]{2,1,0:T(8,128)(2,1)} %shard_map.130), calls=%async_computation | async-start | bytes 1310720 | tf_op jit(solution)/shard_map/all_to_all | solution.py:685
  19.2 21.7 %collective-permute-start.2 = (bf16[256,640]{1,0:T(8,128)(2,1)}, bf16[256,640]{1,0:T(8,128)(2,1)S(1)}, u32[]{:S(2)}, u32[]{:S(2)}) collective-permute-start(bf16[256,640]{1,0:T(8,128)(2,1)} %get-tuple-element.56), channel_id=1, source_target_pairs={{0,2},{1,3},{2,0},{3,1},{4,6},{5,7},{6,4},{7,5},{8,10},{9,11},{10,... | collective-permute-start | bytes 983048 | tf_op jit(solution)/shard_map/ppermute | solution.py:285
  21.0 19.8 %collective-permute-start.3 = (bf16[256,640]{1,0:T(8,128)(2,1)}, bf16[256,640]{1,0:T(8,128)(2,1)S(1)}, u32[]{:S(2)}, u32[]{:S(2)}) collective-permute-start(bf16[256,640]{1,0:T(8,128)(2,1)} %get-tuple-element.57), channel_id=1, source_target_pairs={{0,4},{1,5},{2,6},{3,7},{4,0},{5,1},{6,2},{7,3},{8,12},{9,13},{10,... | collective-permute-start | bytes 983048 | tf_op jit(solution)/shard_map/ppermute | solution.py:285
  22.5 23.2 %collective-permute-start.4 = (bf16[256,640]{1,0:T(8,128)(2,1)}, bf16[256,640]{1,0:T(8,128)(2,1)S(1)}, u32[]{:S(2)}, u32[]{:S(2)}) collective-permute-start(bf16[256,640]{1,0:T(8,128)(2,1)} %get-tuple-element.58), channel_id=1, source_target_pairs={{0,3},{1,2},{2,1},{3,0},{4,7},{5,6},{6,5},{7,4},{8,11},{9,10},{10,... | collective-permute-start | bytes 983048 | tf_op jit(solution)/shard_map/ppermute | solution.py:285
  22.5 8.4 %copy-start.4 = (bf16[256,640]{1,0:T(8,128)(2,1)}, bf16[256,640]{1,0:T(8,128)(2,1)S(1)}, u32[]{:S(2)}) copy-start(bf16[256,640]{1,0:T(8,128)(2,1)S(1)} %collective-permute-done.refs_2_.refs_5_.refs_11_) | copy-start | bytes 983044
  22.5 23.6 %collective-permute-start.5 = (bf16[256,640]{1,0:T(8,128)(2,1)}, bf16[256,640]{1,0:T(8,128)(2,1)S(1)}, u32[]{:S(2)}, u32[]{:S(2)}) collective-permute-start(bf16[256,640]{1,0:T(8,128)(2,1)} %get-tuple-element.59), channel_id=1, source_target_pairs={{0,5},{1,4},{2,7},{3,6},{4,1},{5,0},{6,3},{7,2},{8,13},{9,12},{10,... | collective-permute-start | bytes 983048 | tf_op jit(solution)/shard_map/ppermute | solution.py:285
  29.4 1.5 copy-start.5
  29.4 1.5 copy-start.14
  29.4 16.8 %collective-permute-start.6 = (bf16[256,640]{1,0:T(8,128)(2,1)S(1)}, bf16[256,640]{1,0:T(8,128)(2,1)S(1)}, u32[]{:S(2)}, u32[]{:S(2)}) collective-permute-start(bf16[256,640]{1,0:T(8,128)(2,1)S(1)} %copy-done.16), channel_id=1, source_target_pairs={{0,1},{1,0},{2,3},{3,2},{4,5},{5,4},{6,7},{7,6},{8,9},{9,8},{10,11... | collective-permute-start | bytes 983048 | tf_op jit(solution)/shard_map/ppermute | solution.py:285
  37.2 0.8 copy-start.3
  40.9 5.3 %copy-start.6 = (bf16[256,640]{1,0:T(8,128)(2,1)}, bf16[256,640]{1,0:T(8,128)(2,1)S(1)}, u32[]{:S(2)}) copy-start(bf16[256,640]{1,0:T(8,128)(2,1)S(1)} %collective-permute-done.2.refs_4_.refs_7_.refs_13_) | copy-start | bytes 983044
  40.9 5.3 %copy-start.7 = (bf16[256,640]{1,0:T(8,128)(2,1)}, bf16[256,640]{1,0:T(8,128)(2,1)S(1)}, u32[]{:S(2)}) copy-start(bf16[256,640]{1,0:T(8,128)(2,1)S(1)} %collective-permute-done.3.refs_5_.refs_8_.refs_14_) | copy-start | bytes 983044
  45.7 0.7 copy-start.8
  46.2 0.8 copy-start.10
  49.7 18.5 %collective-permute-start.7 = (bf16[2,256,640]{2,1,0:T(8,128)(2,1)}, bf16[2,256,640]{2,1,0:T(8,128)(2,1)S(1)}, u32[]{:S(2)}, u32[]{:S(2)}) collective-permute-start(bf16[2,256,640]{2,1,0:T(8,128)(2,1)} %shard_map.133.refs_12_), channel_id=1, source_target_pairs={{0,8},{1,9},{2,10},{3,11},{4,12},{5,13},{6,14},{7,15},{8,16},{9,17... | collective-permute-start | bytes 1966088 | tf_op jit(solution)/shard_map/ppermute | solution.py:597
  64.3 21.7 %all-to-all-start.1 = ((bf16[32,16,640]{2,1,0:T(8,128)(2,1)}), bf16[32,16,640]{2,1,0:T(8,128)(2,1)S(1)}, u32[]{:S(2)}, u32[]{:S(2)}) async-start(bf16[32,16,640]{2,1,0:T(8,128)(2,1)} %shard_map.134.refs_3_), calls=%async_computation.1 | async-start | bytes 1310720 | tf_op jit(solution)/shard_map/all_to_all | solution.py:685
  68.1 0.8 copy-start.15
  72.6 4.9 %collective-permute-start.8 = (bf16[144,640]{1,0:T(8,128)(2,1)}, bf16[144,640]{1,0:T(8,128)(2,1)S(1)}, u32[]{:S(2)}, u32[]{:S(2)}) collective-permute-start(bf16[144,640]{1,0:T(8,128)(2,1)} %get-tuple-element.61), channel_id=1, source_target_pairs={{0,1},{1,0},{2,3},{3,2},{4,5},{5,4},{6,7},{7,6},{8,9},{9,8},{10,11... | collective-permute-start | bytes 552968 | tf_op jit(solution)/shard_map/ppermute | solution.py:285
  72.9 10.4 %collective-permute-start.9 = (bf16[144,640]{1,0:T(8,128)(2,1)}, bf16[144,640]{1,0:T(8,128)(2,1)S(1)}, u32[]{:S(2)}, u32[]{:S(2)}) collective-permute-start(bf16[144,640]{1,0:T(8,128)(2,1)} %get-tuple-element.62), channel_id=1, source_target_pairs={{0,6},{1,7},{2,4},{3,5},{4,2},{5,3},{6,0},{7,1},{8,14},{9,15},{10,... | collective-permute-start | bytes 552968 | tf_op jit(solution)/shard_map/ppermute | solution.py:285
  75.5 19.6 %collective-permute-start.10 = (bf16[144,640]{1,0:T(8,128)(2,1)}, bf16[144,640]{1,0:T(8,128)(2,1)S(1)}, u32[]{:S(2)}, u32[]{:S(2)}) collective-permute-start(bf16[144,640]{1,0:T(8,128)(2,1)} %get-tuple-element.65), channel_id=1, source_target_pairs={{0,2},{1,3},{2,0},{3,1},{4,6},{5,7},{6,4},{7,5},{8,10},{9,11},{10,... | collective-permute-start | bytes 552968 | tf_op jit(solution)/shard_map/ppermute | solution.py:285
  76.0 19.1 %collective-permute-start.11 = (bf16[144,640]{1,0:T(8,128)(2,1)}, bf16[144,640]{1,0:T(8,128)(2,1)S(1)}, u32[]{:S(2)}, u32[]{:S(2)}) collective-permute-start(bf16[144,640]{1,0:T(8,128)(2,1)} %get-tuple-element.66), channel_id=1, source_target_pairs={{0,3},{1,2},{2,1},{3,0},{4,7},{5,6},{6,5},{7,4},{8,11},{9,10},{10,... | collective-permute-start | bytes 552968 | tf_op jit(solution)/shard_map/ppermute | solution.py:285
  76.9 18.2 %collective-permute-start.12 = (bf16[144,640]{1,0:T(8,128)(2,1)}, bf16[144,640]{1,0:T(8,128)(2,1)S(1)}, u32[]{:S(2)}, u32[]{:S(2)}) collective-permute-start(bf16[144,640]{1,0:T(8,128)(2,1)} %get-tuple-element.67), channel_id=1, source_target_pairs={{0,4},{1,5},{2,6},{3,7},{4,0},{5,1},{6,2},{7,3},{8,12},{9,13},{10,... | collective-permute-start | bytes 552968 | tf_op jit(solution)/shard_map/ppermute | solution.py:285
  77.5 8.6 %copy-start.11 = (bf16[144,640]{1,0:T(8,128)(2,1)}, bf16[144,640]{1,0:T(8,128)(2,1)S(1)}, u32[]{:S(2)}) copy-start(bf16[144,640]{1,0:T(8,128)(2,1)S(1)} %collective-permute-done.8.refs_5_.refs_3_.refs_6_) | copy-start | bytes 552964
  77.5 17.7 %collective-permute-start.13 = (bf16[144,640]{1,0:T(8,128)(2,1)}, bf16[144,640]{1,0:T(8,128)(2,1)S(1)}, u32[]{:S(2)}, u32[]{:S(2)}) collective-permute-start(bf16[144,640]{1,0:T(8,128)(2,1)} %get-tuple-element.68), channel_id=1, source_target_pairs={{0,5},{1,4},{2,7},{3,6},{4,1},{5,0},{6,3},{7,2},{8,13},{9,12},{10,... | collective-permute-start | bytes 552968 | tf_op jit(solution)/shard_map/ppermute | solution.py:285
  83.3 2.7 %copy-start.12 = (bf16[144,640]{1,0:T(8,128)(2,1)}, bf16[144,640]{1,0:T(8,128)(2,1)S(1)}, u32[]{:S(2)}) copy-start(bf16[144,640]{1,0:T(8,128)(2,1)S(1)} %collective-permute-done.9.refs_6_.refs_8_.refs_11_) | copy-start | bytes 552964
  83.3 12.5 %collective-permute-start.14 = (bf16[144,640]{1,0:T(8,128)(2,1)}, bf16[144,640]{1,0:T(8,128)(2,1)S(1)}, u32[]{:S(2)}, u32[]{:S(2)}) collective-permute-start(bf16[144,640]{1,0:T(8,128)(2,1)} %get-tuple-element.69), channel_id=1, source_target_pairs={{0,7},{1,6},{2,5},{3,4},{4,3},{5,2},{6,1},{7,0},{8,15},{9,14},{10,... | collective-permute-start | bytes 552968 | tf_op jit(solution)/shard_map/ppermute | solution.py:285
  86.0 0.8 copy-start
  90.4 22.4 %all-to-all-start.2 = ((bf16[32,16,640]{2,1,0:T(8,128)(2,1)}), bf16[32,16,640]{2,1,0:T(8,128)(2,1)S(1)}, u32[]{:S(2)}, u32[]{:S(2)}) async-start(bf16[32,16,640]{2,1,0:T(8,128)(2,1)} %get-tuple-element.63.refs_18_), calls=%async_computation.2 | async-start | bytes 1310720 | tf_op jit(solution)/shard_map/all_to_all | solution.py:685
  95.1 0.8 copy-start.17
  95.1 0.8 copy-start.18
  95.1 0.8 copy-start.19
  95.1 0.9 copy-start.20
  107.8 8.4 %collective-permute-start.15 = (bf16[128,640]{1,0:T(8,128)(2,1)}, bf16[128,640]{1,0:T(8,128)(2,1)S(1)}, u32[]{:S(2)}, u32[]{:S(2)}) collective-permute-start(bf16[128,640]{1,0:T(8,128)(2,1)} %get-tuple-element.76), channel_id=1, source_target_pairs={{0,1},{1,0},{2,3},{3,2},{4,5},{5,4},{6,7},{7,6},{8,9},{9,8},{10,11... | collective-permute-start | bytes 491528 | tf_op jit(solution)/shard_map/ppermute | solution.py:285
  107.9 10.7 %collective-permute-start.16 = (bf16[128,640]{1,0:T(8,128)(2,1)}, bf16[128,640]{1,0:T(8,128)(2,1)S(1)}, u32[]{:S(2)}, u32[]{:S(2)}) collective-permute-start(bf16[128,640]{1,0:T(8,128)(2,1)} %get-tuple-element.77), channel_id=1, source_target_pairs={{0,2},{1,3},{2,0},{3,1},{4,6},{5,7},{6,4},{7,5},{8,10},{9,11},{10,... | collective-permute-start | bytes 491528 | tf_op jit(solution)/shard_map/ppermute | solution.py:285
  109.1 17.8 %collective-permute-start.17 = (bf16[128,640]{1,0:T(8,128)(2,1)}, bf16[128,640]{1,0:T(8,128)(2,1)S(1)}, u32[]{:S(2)}, u32[]{:S(2)}) collective-permute-start(bf16[128,640]{1,0:T(8,128)(2,1)} %get-tuple-element.78), channel_id=1, source_target_pairs={{0,3},{1,2},{2,1},{3,0},{4,7},{5,6},{6,5},{7,4},{8,11},{9,10},{10,... | collective-permute-start | bytes 491528 | tf_op jit(solution)/shard_map/ppermute | solution.py:285
  109.7 19.0 %collective-permute-start.18 = (bf16[128,640]{1,0:T(8,128)(2,1)}, bf16[128,640]{1,0:T(8,128)(2,1)S(1)}, u32[]{:S(2)}, u32[]{:S(2)}) collective-permute-start(bf16[128,640]{1,0:T(8,128)(2,1)} %get-tuple-element.79), channel_id=1, source_target_pairs={{0,4},{1,5},{2,6},{3,7},{4,0},{5,1},{6,2},{7,3},{8,12},{9,13},{10,... | collective-permute-start | bytes 491528 | tf_op jit(solution)/shard_map/ppermute | solution.py:285
  110.8 19.3 %collective-permute-start.19 = (bf16[128,640]{1,0:T(8,128)(2,1)}, bf16[128,640]{1,0:T(8,128)(2,1)S(1)}, u32[]{:S(2)}, u32[]{:S(2)}) collective-permute-start(bf16[128,640]{1,0:T(8,128)(2,1)} %get-tuple-element.80), channel_id=1, source_target_pairs={{0,5},{1,4},{2,7},{3,6},{4,1},{5,0},{6,3},{7,2},{8,13},{9,12},{10,... | collective-permute-start | bytes 491528 | tf_op jit(solution)/shard_map/ppermute | solution.py:285
  112.8 0.8 copy-start.1
  116.2 10.7 %copy-start.22 = (bf16[128,640]{1,0:T(8,128)(2,1)}, bf16[128,640]{1,0:T(8,128)(2,1)S(1)}, u32[]{:S(2)}) copy-start(bf16[128,640]{1,0:T(8,128)(2,1)S(1)} %collective-permute-done.15.refs_13_.refs_11_) | copy-start | bytes 491524
  116.2 14.0 %collective-permute-start.20 = (bf16[128,640]{1,0:T(8,128)(2,1)}, bf16[128,640]{1,0:T(8,128)(2,1)S(1)}, u32[]{:S(2)}, u32[]{:S(2)}) collective-permute-start(bf16[128,640]{1,0:T(8,128)(2,1)} %get-tuple-element.81), channel_id=1, source_target_pairs={{0,6},{1,7},{2,4},{3,5},{4,2},{5,3},{6,0},{7,1},{8,14},{9,15},{10,... | collective-permute-start | bytes 491528 | tf_op jit(solution)/shard_map/ppermute | solution.py:285
  118.5 8.4 %copy-start.23 = (bf16[128,640]{1,0:T(8,128)(2,1)}, bf16[128,640]{1,0:T(8,128)(2,1)S(1)}, u32[]{:S(2)}) copy-start(bf16[128,640]{1,0:T(8,128)(2,1)S(1)} %collective-permute-done.16.refs_14_.refs_12_) | copy-start | bytes 491524
  118.5 12.9 %collective-permute-start.21 = (bf16[128,640]{1,0:T(8,128)(2,1)}, bf16[128,640]{1,0:T(8,128)(2,1)S(1)}, u32[]{:S(2)}, u32[]{:S(2)}) collective-permute-start(bf16[128,640]{1,0:T(8,128)(2,1)} %get-tuple-element.82), channel_id=1, source_target_pairs={{0,7},{1,6},{2,5},{3,4},{4,3},{5,2},{6,1},{7,0},{8,15},{9,14},{10,... | collective-permute-start | bytes 491528 | tf_op jit(solution)/shard_map/ppermute | solution.py:285
  127.0 6.1 %copy-start.24 = (bf16[128,640]{1,0:T(8,128)(2,1)}, bf16[128,640]{1,0:T(8,128)(2,1)S(1)}, u32[]{:S(2)}) copy-start(bf16[128,640]{1,0:T(8,128)(2,1)S(1)} %collective-permute-done.17.refs_15_.refs_13_) | copy-start | bytes 491524
  127.0 20.1 %collective-permute-start.22 = (bf16[128,640]{1,0:T(8,128)(2,1)}, bf16[128,640]{1,0:T(8,128)(2,1)S(1)}, u32[]{:S(2)}, u32[]{:S(2)}) collective-permute-start(bf16[128,640]{1,0:T(8,128)(2,1)} %get-tuple-element.83), channel_id=1, source_target_pairs={{0,3},{1,2},{2,1},{3,0},{4,7},{5,6},{6,5},{7,4},{8,11},{9,10},{10,... | collective-permute-start | bytes 491528 | tf_op jit(solution)/shard_map/ppermute | solution.py:285
  128.7 4.4 %copy-start.25 = (bf16[128,640]{1,0:T(8,128)(2,1)}, bf16[128,640]{1,0:T(8,128)(2,1)S(1)}, u32[]{:S(2)}) copy-start(bf16[128,640]{1,0:T(8,128)(2,1)S(1)} %collective-permute-done.18.refs_16_.refs_14_) | copy-start | bytes 491524
  128.7 18.4 %collective-permute-start.23 = (bf16[128,640]{1,0:T(8,128)(2,1)}, bf16[128,640]{1,0:T(8,128)(2,1)S(1)}, u32[]{:S(2)}, u32[]{:S(2)}) collective-permute-start(bf16[128,640]{1,0:T(8,128)(2,1)} %get-tuple-element.84), channel_id=1, source_target_pairs={{0,4},{1,5},{2,6},{3,7},{4,0},{5,1},{6,2},{7,3},{8,12},{9,13},{10,... | collective-permute-start | bytes 491528 | tf_op jit(solution)/shard_map/ppermute | solution.py:285
  130.2 2.9 %copy-start.26 = (bf16[128,640]{1,0:T(8,128)(2,1)}, bf16[128,640]{1,0:T(8,128)(2,1)S(1)}, u32[]{:S(2)}) copy-start(bf16[128,640]{1,0:T(8,128)(2,1)S(1)} %collective-permute-done.19.refs_17_.refs_15_) | copy-start | bytes 491524
  130.2 17.0 %collective-permute-start.24 = (bf16[128,640]{1,0:T(8,128)(2,1)}, bf16[128,640]{1,0:T(8,128)(2,1)S(1)}, u32[]{:S(2)}, u32[]{:S(2)}) collective-permute-start(bf16[128,640]{1,0:T(8,128)(2,1)} %get-tuple-element.85), channel_id=1, source_target_pairs={{0,5},{1,4},{2,7},{3,6},{4,1},{5,0},{6,3},{7,2},{8,13},{9,12},{10,... | collective-permute-start | bytes 491528 | tf_op jit(solution)/shard_map/ppermute | solution.py:285
  130.2 2.9 %copy-start.27 = (bf16[128,640]{1,0:T(8,128)(2,1)}, bf16[128,640]{1,0:T(8,128)(2,1)S(1)}, u32[]{:S(2)}) copy-start(bf16[128,640]{1,0:T(8,128)(2,1)S(1)} %collective-permute-done.20.refs_18_.refs_16_) | copy-start | bytes 491524
  130.2 16.9 %collective-permute-start.25 = (bf16[128,640]{1,0:T(8,128)(2,1)}, bf16[128,640]{1,0:T(8,128)(2,1)S(1)}, u32[]{:S(2)}, u32[]{:S(2)}) collective-permute-start(bf16[128,640]{1,0:T(8,128)(2,1)} %get-tuple-element.86), channel_id=1, source_target_pairs={{0,6},{1,7},{2,4},{3,5},{4,2},{5,3},{6,0},{7,1},{8,14},{9,15},{10,... | collective-permute-start | bytes 491528 | tf_op jit(solution)/shard_map/ppermute | solution.py:285
  131.5 1.6 copy-start.28
  131.5 15.7 %collective-permute-start.26 = (bf16[128,640]{1,0:T(8,128)(2,1)}, bf16[128,640]{1,0:T(8,128)(2,1)S(1)}, u32[]{:S(2)}, u32[]{:S(2)}) collective-permute-start(bf16[128,640]{1,0:T(8,128)(2,1)} %get-tuple-element.87), channel_id=1, source_target_pairs={{0,7},{1,6},{2,5},{3,4},{4,3},{5,2},{6,1},{7,0},{8,15},{9,14},{10,... | collective-permute-start | bytes 491528 | tf_op jit(solution)/shard_map/ppermute | solution.py:285
  137.9 27.2 %all-to-all-start.3 = ((bf16[32,16,640]{2,1,0:T(8,128)(2,1)}), bf16[32,16,640]{2,1,0:T(8,128)(2,1)S(1)}, u32[]{:S(2)}, u32[]{:S(2)}) async-start(bf16[32,16,640]{2,1,0:T(8,128)(2,1)} %shard_map.140.refs_3_), calls=%async_computation.3 | async-start | bytes 1310720 | tf_op jit(solution)/shard_map/all_to_all | solution.py:685
  147.1 0.7 copy-start.30
  147.1 0.8 copy-start.31
  147.2 0.8 copy-start.32
  147.2 0.8 copy-start.33
  148.0 4.5 %copy-start.13 = (f32[2560]{0:T(1024)S(1)}, f32[2560]{0:T(1024)}, u32[]{:S(2)}) copy-start(f32[2560]{0:T(1024)} %param.19) | copy-start | bytes 30724
  150.6 17.6 %collective-permute-start.27 = (bf16[128,640]{1,0:T(8,128)(2,1)}, bf16[128,640]{1,0:T(8,128)(2,1)S(1)}, u32[]{:S(2)}, u32[]{:S(2)}) collective-permute-start(bf16[128,640]{1,0:T(8,128)(2,1)} %get-tuple-element.88.refs_5_), channel_id=1, source_target_pairs={{0,1},{1,0},{2,3},{3,2},{4,5},{5,4},{6,7},{7,6},{8,9},{9,8},{10,11... | collective-permute-start | bytes 491528 | tf_op jit(solution)/shard_map/ppermute | solution.py:285
  150.9 17.3 %collective-permute-start.28 = (bf16[128,640]{1,0:T(8,128)(2,1)}, bf16[128,640]{1,0:T(8,128)(2,1)S(1)}, u32[]{:S(2)}, u32[]{:S(2)}) collective-permute-start(bf16[128,640]{1,0:T(8,128)(2,1)} %get-tuple-element.89), channel_id=1, source_target_pairs={{0,2},{1,3},{2,0},{3,1},{4,6},{5,7},{6,4},{7,5},{8,10},{9,11},{10,... | collective-permute-start | bytes 491528 | tf_op jit(solution)/shard_map/ppermute | solution.py:285
  165.0 0.8 copy-start.2
  (5 other events, 3.5 us)
where the time goes:
time: 175 us; the launch traced here: 174 us
  Pallas kernels  67.9 us (39%)
  starting transfers between devices  56.5 us (32%)
  waiting for transfers between devices  38 us (22%)
  local copies, waits for them, and re-layouts  7.36 us (4%)
  other arithmetic  1.91 us (1%)
  between operations  1.86 us (1%)
    pallas_call x15, Pallas kernels, call(): pl.pallas_call(kernel, out_shape=(*outputs, *far), in_specs=[SMEM] + [VME...  67.9 us
    ppermute x28, starting transfers between devices, exchange(): lax.ppermute(blocks[step], 'tok', pairs)  29.1 us
    all_to_all x4, starting transfers between devices, spread(): return lax.all_to_all(wire, 'tok', 0, 0, tiled=True)  23.7 us
    all_to_all x4, waiting for transfers between devices, spread(): return lax.all_to_all(wire, 'tok', 0, 0, tiled=True)  20.9 us
    ppermute x28, waiting for transfers between devices, exchange(): lax.ppermute(blocks[step], 'tok', pairs)  17.1 us
    unnamed x72, local copies, waits for them, and re-layouts  7.28 us
    ppermute x1, starting transfers between devices, halo_of(): return lax.ppermute(last, 'tok', pairs)  3.71 us
  transfers between devices with their start and end apart: 33, of which 10 were waited for; matrix products, arithmetic and copies ran while one was open for 1% of the time, Pallas kernels for 33%

commit v1 on v0

--- a/solution.py
+++ b/solution.py
@@ -729,11 +729,11 @@
     if later:
         after = delayed(plan, info, part(later, found), (wire, *part(first[1:], mixed)))
         mixed.update(exchange(plan, dict(zip(later, after)), later))
-    states = update(plan, info, states, spread(wire), False, after[:1])
     if plan.group > 1:
-        output = finish(plan, info, mixed, attended, gain, states[:1])
+        output = finish(plan, info, mixed, attended, gain, after[:1])
     else:
         output = finish_apart(plan, mixed, attended, gain)
+    states = update(plan, info, states, spread(wire), False, (output,))
     return (output, *(jnp.transpose(w, (1, 2, 0)) for w in states))
 
 

time: 175 us -> 170 us (0.971)
  waiting for transfers between devices: 38 us -> 33.3 us
    all_to_all x4, waiting for transfers between devices: 20.9 us -> 9.28 us  [spread(): return lax.all_to_all(wire, 'tok', 0, 0, tiled=True)]
    ppermute x28, waiting for transfers between devices: 17.1 us -> 24 us  [exchange(): lax.ppermute(blocks[step], 'tok', pairs)]
  transfers between devices with their start and end apart: 33 -> 33, of which waited for: 10 -> 10; matrix products, arithmetic and copies ran while one was open for 1% -> 1% of each run, Pallas kernels for 33% -> 35%
where the time goes in v1:
time: 170 us; the launch traced here: 169 us
  Pallas kernels  67.9 us (40%)
  starting transfers between devices  56.5 us (33%)
  waiting for transfers between devices  33.3 us (20%)
  local copies, waits for them, and re-layouts  7.37 us (4%)
  other arithmetic  1.9 us (1%)
  between operations  1.85 us (1%)
    pallas_call x15, Pallas kernels, call(): pl.pallas_call(kernel, out_shape=(*outputs, *far), in_specs=[SMEM] + [VME...  67.9 us
    ppermute x28, starting transfers between devices, exchange(): lax.ppermute(blocks[step], 'tok', pairs)  29 us
    ppermute x28, waiting for transfers between devices, exchange(): lax.ppermute(blocks[step], 'tok', pairs)  24 us
    all_to_all x4, starting transfers between devices, spread(): return lax.all_to_all(wire, 'tok', 0, 0, tiled=True)  23.8 us
    all_to_all x4, waiting for transfers between devices, spread(): return lax.all_to_all(wire, 'tok', 0, 0, tiled=True)  9.28 us
    unnamed x72, local copies, waits for them, and re-layouts  7.3 us
    ppermute x1, starting transfers between devices, halo_of(): return lax.ppermute(last, 'tok', pairs)  3.71 us
  transfers between devices with their start and end apart: 33, of which 10 were waited for; matrix products, arithmetic and copies ran while one was open for 1% of the time, Pallas kernels for 35%

profile of v1, /device:TPU:0, one launch (start us, length us, event | category | flops | bytes accessed | tf_op | source)
XLA Modules:
  0.0 168.8 jit_solution(12955115228646003115)
XLA Ops:
  1.3 0.7 pad_add_fusion.refs_0_
  1.9 4.3 %shard_map.129 = (bf16[256,640]{1,0:T(8,128)(2,1)}, bf16[256,640]{1,0:T(8,128)(2,1)}, bf16[256,640]{1,0:T(8,128)(2,1)}, bf16[256,640]{1,0:T(8,128)(2,1)}, bf16[2...) custom-call(s32[4]{0:T(128)} %pad_add_fusion.refs_0_, ...), custom_call_target="tpu_custom_call" | custom-call | tf_op jit(solution)/shard_map/pallas_call | solution.py:39
  6.3 4.0 %collective-permute-start = (bf16[256,640]{1,0:T(8,128)(2,1)}, bf16[256,640]{1,0:T(8,128)(2,1)S(1)}, u32[]{:S(2)}, u32[]{:S(2)}) collective-permute-start(bf16[256,640]{1,0:T(8,128)(2,1)} %get-tuple-element.54), channel_id=1, source_target_pairs={{0,6},{1,7},{2,4},{3,5},{4,2},{5,3},{6,0},{7,1},{8,14},{9,15},{10,... | collective-permute-start | bytes 983048 | tf_op jit(solution)/shard_map/ppermute | solution.py:285
  10.2 2.9 %shard_map.130 = bf16[32,16,640]{2,1,0:T(8,128)(2,1)} custom-call(s32[4]{0:T(128)} %pad_add_fusion.refs_0_, f32[10,8,320]{2,1,0:T(8,128)} %bitcast.11, f32[10,8,320]{2,1,0:T(8,128)} %bitcast.13, f32[10,8,320]{2,1,0:T(8,128)} %bitcast.15, f32[8,256]{1,0:T(8,128)} %bitcast.17, bf16[256,640]{1,0:T(8,128)(2,1)} %get-tuple-element.50.refs_5_.refs_1_.refs_4_.refs_10_), custom_call_target="tpu_custom_call" | custom-call | tf_op jit(solution)/shard_map/pallas_call | solution.py:39
  13.2 6.1 %all-to-all-start = ((bf16[32,16,640]{2,1,0:T(8,128)(2,1)}), bf16[32,16,640]{2,1,0:T(8,128)(2,1)S(1)}, u32[]{:S(2)}, u32[]{:S(2)}) async-start(bf16[32,16,640]{2,1,0:T(8,128)(2,1)} %shard_map.130), calls=%async_computation | async-start | bytes 1310720 | tf_op jit(solution)/shard_map/all_to_all | solution.py:685
  19.2 1.8 %collective-permute-start.2 = (bf16[256,640]{1,0:T(8,128)(2,1)}, bf16[256,640]{1,0:T(8,128)(2,1)S(1)}, u32[]{:S(2)}, u32[]{:S(2)}) collective-permute-start(bf16[256,640]{1,0:T(8,128)(2,1)} %get-tuple-element.56), channel_id=1, source_target_pairs={{0,2},{1,3},{2,0},{3,1},{4,6},{5,7},{6,4},{7,5},{8,10},{9,11},{10,... | collective-permute-start | bytes 983048 | tf_op jit(solution)/shard_map/ppermute | solution.py:285
  21.0 1.5 collective-permute-start.3
  22.5 0.5 collective-permute-start.5
  23.1 6.3 %collective-permute-done.1.refs_3_.refs_6_.refs_12_ = bf16[256,640]{1,0:T(8,128)(2,1)S(1)} collective-permute-done((bf16[256,640]{1,0:T(8,128)(2,1)}, bf16[256,640]{1,0:T(8,128)(2,1)S(1)}, u32[]{:S(2)}, u32[]{:S(2)}) %collective-permute-start.1) | collective-permute-done | bytes 327712 | tf_op jit(solution)/shard_map/ppermute | solution.py:285
  29.6 1.3 shard_map.131.refs_2_
  30.9 0.6 convert_element_type.3
  31.5 5.7 %all-to-all-done.refs_1_ = bf16[32,16,640]{2,1,0:T(8,128)(2,1)S(1)} async-done(((bf16[32,16,640]{2,1,0:T(8,128)(2,1)}), bf16[32,16,640]{2,1,0:T(8,128)(2,1)S(1)}, u32[]{:S(2)}, u32[]{:S(2)}) %all-to-all-start) | async-done | bytes 655392 | tf_op jit(solution)/shard_map/all_to_all | solution.py:685
  37.2 0.8 copy-done.3
  38.0 2.5 %shard_map.132 = (bf16[384,768]{1,0:T(8,128)(2,1)}, bf16[384,384]{1,0:T(8,128)(2,1)}, f32[8,256]{1,0:T(8,128)}) custom-call(s32[4]{0:T(128)} %pad_add_fusion.refs_0_, bf16[32,16,640]{2,1,0:T(8,128)(2,1)} %copy-done.3, s32[8,128]{1,0:T(8,128)} %shard_map.131.refs_2_), custom_call_target="tpu_custom_call" | custom-call | tf_op jit(solution)/shard_map/pallas_call | solution.py:39
  40.5 0.4 collective-permute-done.2.refs_4_.refs_7_.refs_13_
  40.9 4.9 %collective-permute-done.4.refs_6_.refs_9_.refs_15_ = bf16[256,640]{1,0:T(8,128)(2,1)S(1)} collective-permute-done((bf16[256,640]{1,0:T(8,128)(2,1)}, bf16[256,640]{1,0:T(8,128)(2,1)S(1)}, u32[]{:S(2)}, u32[]{:S(2)}) %collective-permute-start.4) | collective-permute-done | bytes 327712 | tf_op jit(solution)/shard_map/ppermute | solution.py:285
  45.7 0.4 collective-permute-done.5.refs_7_.refs_10_.refs_16_
  46.5 0.4 copy-done.9
  47.0 2.7 %shard_map.133.refs_12_ = bf16[2,256,640]{2,1,0:T(8,128)(2,1)} custom-call(s32[4]{0:T(128)} %pad_add_fusion.refs_0_, bf16[256,640]{1,0:T(8,128)(2,1)} %get-tuple-element.50.refs_5_.refs_1_.refs_4_.refs_10_, bf16[256,640]{1,0:T(8,128)(2,1)} %copy-done.4, bf16[256,640]{1,0:T(8,128)(2,1)} %copy-done.5, bf16[256,640]{1,0:T(8,128)(2,1)} %copy-done.6, ...), custom_call_target="tpu_custom_call" | custom-call | tf_op jit(solution)/shard_map/pallas_call | solution.py:39
  49.7 3.7 %collective-permute-start.7 = (bf16[2,256,640]{2,1,0:T(8,128)(2,1)}, bf16[2,256,640]{2,1,0:T(8,128)(2,1)S(1)}, u32[]{:S(2)}, u32[]{:S(2)}) collective-permute-start(bf16[2,256,640]{2,1,0:T(8,128)(2,1)} %shard_map.133.refs_12_), channel_id=1, source_target_pairs={{0,8},{1,9},{2,10},{3,11},{4,12},{5,13},{6,14},{7,15},{8,16},{9,17... | collective-permute-start | bytes 1966088 | tf_op jit(solution)/shard_map/ppermute | solution.py:597
  53.4 10.9 %shard_map.134.refs_3_ = bf16[32,16,640]{2,1,0:T(8,128)(2,1)} custom-call(s32[4]{0:T(128)} %pad_add_fusion.refs_0_, f32[8,256]{1,0:T(8,128)} %get-tuple-element.53.refs_1_, bf16[384,768]{1,0:T(8,128)(2,1)} %get-tuple-element.51.refs_2_.refs_1_, bf16[384,384]{1,0:T(8,128)(2,1)} %get-tuple-element.52.refs_9_.refs_3_.refs_2_, ...), custom_call_target="tpu_custom_call" | custom-call | flops 12000000000 | tf_op jit(solution)/shard_map/pallas_call | solution.py:39
  64.3 3.8 %all-to-all-start.1 = ((bf16[32,16,640]{2,1,0:T(8,128)(2,1)}), bf16[32,16,640]{2,1,0:T(8,128)(2,1)S(1)}, u32[]{:S(2)}, u32[]{:S(2)}) async-start(bf16[32,16,640]{2,1,0:T(8,128)(2,1)} %shard_map.134.refs_3_), calls=%async_computation.1 | async-start | bytes 1310720 | tf_op jit(solution)/shard_map/all_to_all | solution.py:685
  68.1 0.9 copy-done.15
  69.0 3.6 %shard_map.135 = (bf16[144,640]{1,0:T(8,128)(2,1)}, bf16[144,640]{1,0:T(8,128)(2,1)}, bf16[144,640]{1,0:T(8,128)(2,1)}, bf16[144,640]{1,0:T(8,128)(2,1)}, bf16[1...) custom-call(s32[4]{0:T(128)} %pad_add_fusion.refs_0_, ...), custom_call_target="tpu_custom_call" | custom-call | flops 30000001024 | tf_op jit(solution)/shard_map/pallas_call | solution.py:39
  72.6 0.3 collective-permute-start.8
  72.9 2.6 %collective-permute-start.9 = (bf16[144,640]{1,0:T(8,128)(2,1)}, bf16[144,640]{1,0:T(8,128)(2,1)S(1)}, u32[]{:S(2)}, u32[]{:S(2)}) collective-permute-start(bf16[144,640]{1,0:T(8,128)(2,1)} %get-tuple-element.62), channel_id=1, source_target_pairs={{0,6},{1,7},{2,4},{3,5},{4,2},{5,3},{6,0},{7,1},{8,14},{9,15},{10,... | collective-permute-start | bytes 552968 | tf_op jit(solution)/shard_map/ppermute | solution.py:285
  75.5 0.6 collective-permute-start.10
  76.1 0.9 collective-permute-start.11
  77.0 0.6 collective-permute-start.12
  77.5 1.5 collective-permute-start.13
  79.0 4.3 %collective-permute-done.9.refs_6_.refs_8_.refs_11_ = bf16[144,640]{1,0:T(8,128)(2,1)S(1)} collective-permute-done((bf16[144,640]{1,0:T(8,128)(2,1)}, bf16[144,640]{1,0:T(8,128)(2,1)S(1)}, u32[]{:S(2)}, u32[]{:S(2)}) %collective-permute-start.9) | collective-permute-done | bytes 184352 | tf_op jit(solution)/shard_map/ppermute | solution.py:285
  83.4 0.5 collective-permute-start.14
  83.9 2.1 %all-to-all-done.1.refs_1_ = bf16[32,16,640]{2,1,0:T(8,128)(2,1)S(1)} async-done(((bf16[32,16,640]{2,1,0:T(8,128)(2,1)}), bf16[32,16,640]{2,1,0:T(8,128)(2,1)S(1)}, u32[]{:S(2)}, u32[]{:S(2)}) %all-to-all-start.1) | async-done | bytes 655392 | tf_op jit(solution)/shard_map/all_to_all | solution.py:685
  86.1 0.8 copy-done.1
  86.9 3.6 %shard_map.136 = (f32[10,8,320]{2,1,0:T(8,128)}, f32[10,8,320]{2,1,0:T(8,128)}, f32[10,8,320]{2,1,0:T(8,128)}, bf16[32,16,640]{2,1,0:T(8,128)(2,1)}) custom-call(s32[4]{0:T(128)} %pad_add_fusion.refs_0_, bf16[32,16,640]{2,1,0:T(8,128)(2,1)} %copy-done.1, f32[10,8,320]{2,1,0:T(8,128)} %bitcast.12, f32[10,8,320]{2,1,0:T(8,128)} %bitcast.14, ...), custom_call_target="tpu_custom_call" | custom-call | tf_op jit(solution)/shard_map/pallas_call | solution.py:39
  90.5 4.6 %all-to-all-start.2 = ((bf16[32,16,640]{2,1,0:T(8,128)(2,1)}), bf16[32,16,640]{2,1,0:T(8,128)(2,1)S(1)}, u32[]{:S(2)}, u32[]{:S(2)}) async-start(bf16[32,16,640]{2,1,0:T(8,128)(2,1)} %get-tuple-element.63.refs_18_), calls=%async_computation.2 | async-start | bytes 1310720 | tf_op jit(solution)/shard_map/all_to_all | solution.py:685
  95.2 0.7 collective-permute-done.14.refs_9_.refs_12_
  96.0 0.6 copy-done.21
  96.6 11.2 %shard_map.137 = (bf16[128,640]{1,0:T(8,128)(2,1)}, bf16[128,640]{1,0:T(8,128)(2,1)}, bf16[128,640]{1,0:T(8,128)(2,1)}, bf16[128,640]{1,0:T(8,128)(2,1)}, bf16[1...) custom-call(s32[4]{0:T(128)} %pad_add_fusion.refs_0_, ...), custom_call_target="tpu_custom_call" | custom-call | flops 10000000000 | tf_op jit(solution)/shard_map/pallas_call | solution.py:39
  108.0 1.2 collective-permute-start.16
  109.2 0.6 collective-permute-start.17
  109.8 1.1 collective-permute-start.18
  110.9 0.6 collective-permute-start.19
  111.5 1.5 all-to-all-done.2.refs_1_
  113.0 0.8 copy-done.2
  113.8 2.5 %shard_map.138 = (bf16[384,768]{1,0:T(8,128)(2,1)}, bf16[384,384]{1,0:T(8,128)(2,1)}, f32[8,256]{1,0:T(8,128)}) custom-call(s32[4]{0:T(128)} %pad_add_fusion.refs_0_, bf16[32,16,640]{2,1,0:T(8,128)(2,1)} %copy-done.2, bf16[128,640]{1,0:T(8,128)(2,1)} %get-tuple-element.70.refs_2_.refs_10_), custom_call_target="tpu_custom_call" | custom-call | tf_op jit(solution)/shard_map/pallas_call | solution.py:39
  116.3 2.2 %collective-permute-start.20 = (bf16[128,640]{1,0:T(8,128)(2,1)}, bf16[128,640]{1,0:T(8,128)(2,1)S(1)}, u32[]{:S(2)}, u32[]{:S(2)}) collective-permute-start(bf16[128,640]{1,0:T(8,128)(2,1)} %get-tuple-element.81), channel_id=1, source_target_pairs={{0,6},{1,7},{2,4},{3,5},{4,2},{5,3},{6,0},{7,1},{8,14},{9,15},{10,... | collective-permute-start | bytes 491528 | tf_op jit(solution)/shard_map/ppermute | solution.py:285
  118.6 8.3 %shard_map.139 = (bf16[128,640]{1,0:T(8,128)(2,1)}, bf16[128,640]{1,0:T(8,128)(2,1)}, bf16[128,640]{1,0:T(8,128)(2,1)}, bf16[128,640]{1,0:T(8,128)(2,1)}, bf16[1...) custom-call(s32[4]{0:T(128)} %pad_add_fusion.refs_0_, ...), custom_call_target="tpu_custom_call" | custom-call | flops 8000000000 | tf_op jit(solution)/shard_map/pallas_call | solution.py:39
  126.9 1.7 %collective-permute-start.22 = (bf16[128,640]{1,0:T(8,128)(2,1)}, bf16[128,640]{1,0:T(8,128)(2,1)S(1)}, u32[]{:S(2)}, u32[]{:S(2)}) collective-permute-start(bf16[128,640]{1,0:T(8,128)(2,1)} %get-tuple-element.83), channel_id=1, source_target_pairs={{0,3},{1,2},{2,1},{3,0},{4,7},{5,6},{6,5},{7,4},{8,11},{9,10},{10,... | collective-permute-start | bytes 491528 | tf_op jit(solution)/shard_map/ppermute | solution.py:285
  128.7 1.5 collective-permute-start.23
  130.2 1.2 collective-permute-start.25
  131.4 1.6 collective-permute-start.26
  133.1 4.8 %shard_map.140.refs_3_ = bf16[32,16,640]{2,1,0:T(8,128)(2,1)} custom-call(s32[4]{0:T(128)} %pad_add_fusion.refs_0_, f32[8,256]{1,0:T(8,128)} %get-tuple-element.53.refs_1_, bf16[384,768]{1,0:T(8,128)(2,1)} %get-tuple-element.71.refs_3_.refs_2_, bf16[384,384]{1,0:T(8,128)(2,1)} %get-tuple-element.72.refs_4_.refs_3_, ...), custom_call_target="tpu_custom_call" | custom-call | flops 12000000000 | tf_op jit(solution)/shard_map/pallas_call | solution.py:39
  137.8 9.3 %all-to-all-start.3 = ((bf16[32,16,640]{2,1,0:T(8,128)(2,1)}), bf16[32,16,640]{2,1,0:T(8,128)(2,1)S(1)}, u32[]{:S(2)}, u32[]{:S(2)}) async-start(bf16[32,16,640]{2,1,0:T(8,128)(2,1)} %shard_map.140.refs_3_), calls=%async_computation.3 | async-start | bytes 1310720 | tf_op jit(solution)/shard_map/all_to_all | solution.py:685
  147.3 0.6 copy-done.29
  148.1 2.5 %shard_map.141 = (bf16[128,640]{1,0:T(8,128)(2,1)}, bf16[128,640]{1,0:T(8,128)(2,1)}) custom-call(s32[4]{0:T(128)} %pad_add_fusion.refs_0_, bf16[128,640]{1,0:T(8,128)(2,1)} %get-tuple-element.74.refs_1_, bf16[128,640]{1,0:T(8,128)(2,1)} %get-tuple-element.75.refs_2_, bf16[32,16,640]{2,1,0:T(8,128)(2,1)} %shard_map.140.refs_3_, bf16[128,640]{1,0:T(8,128)(2,1)} %copy-done.29, ...), custom_call_target="tpu_custom_call" | custom-call | flops 20000000000 | tf_op jit(solution)/shard_map/pallas_call | solution.py:39
  150.6 0.3 collective-permute-start.27
  150.9 1.7 collective-permute-start.28
  152.7 0.7 pad_maximum_fusion.refs_1_
  153.4 6.9 %collective-permute-done.28.refs_4_ = bf16[128,640]{1,0:T(8,128)(2,1)S(1)} collective-permute-done((bf16[128,640]{1,0:T(8,128)(2,1)}, bf16[128,640]{1,0:T(8,128)(2,1)S(1)}, u32[]{:S(2)}, u32[]{:S(2)}) %collective-permute-start.28) | collective-permute-done | bytes 163872 | tf_op jit(solution)/shard_map/ppermute | solution.py:285
  160.3 0.7 copy-done.35
  161.0 4.5 %shard_map.142.refs_5_ = bf16[256,2560]{1,0:T(8,128)(2,1)} custom-call(s32[4]{0:T(128)} %pad_add_fusion.refs_0_, f32[8,640]{1,0:T(8,128)} %pad_maximum_fusion.refs_1_, bf16[128,640]{1,0:T(8,128)(2,1)} %get-tuple-element.73.refs_12_.refs_2_, bf16[128,640]{1,0:T(8,128)(2,1)} %copy-done.34, bf16[128,640]{1,0:T(8,128)(2,1)} %copy-done.35, ...), custom_call_target="tpu_custom_call" | custom-call | flops 10000000000 | tf_op jit(solution)/shard_map/pallas_call | solution.py:39
  165.5 0.8 copy-done
  166.3 2.3 %shard_map.143 = (f32[10,8,320]{2,1,0:T(8,128)}, f32[10,8,320]{2,1,0:T(8,128)}, f32[10,8,320]{2,1,0:T(8,128)}) custom-call(s32[4]{0:T(128)} %pad_add_fusion.refs_0_, bf16[32,16,640]{2,1,0:T(8,128)(2,1)} %copy-done, f32[10,8,320]{2,1,0:T(8,128)} %get-tuple-element.90.refs_2_, f32[10,8,320]{2,1,0:T(8,128)} %get-tuple-element.91.refs_3_, ...), custom_call_target="tpu_custom_call" | custom-call | tf_op jit(solution)/shard_map/pallas_call | solution.py:39
  (93 shorter events, 1.4 us)
Async XLA Ops:
  6.3 16.3 %collective-permute-start = (bf16[256,640]{1,0:T(8,128)(2,1)}, bf16[256,640]{1,0:T(8,128)(2,1)S(1)}, u32[]{:S(2)}, u32[]{:S(2)}) collective-permute-start(bf16[256,640]{1,0:T(8,128)(2,1)} %get-tuple-element.54), channel_id=1, source_target_pairs={{0,6},{1,7},{2,4},{3,5},{4,2},{5,3},{6,0},{7,1},{8,14},{9,15},{10,... | collective-permute-start | bytes 983048 | tf_op jit(solution)/shard_map/ppermute | solution.py:285
  10.2 19.2 %collective-permute-start.1 = (bf16[256,640]{1,0:T(8,128)(2,1)}, bf16[256,640]{1,0:T(8,128)(2,1)S(1)}, u32[]{:S(2)}, u32[]{:S(2)}) collective-permute-start(bf16[256,640]{1,0:T(8,128)(2,1)} %get-tuple-element.55), channel_id=1, source_target_pairs={{0,7},{1,6},{2,5},{3,4},{4,3},{5,2},{6,1},{7,0},{8,15},{9,14},{10,... | collective-permute-start | bytes 983048 | tf_op jit(solution)/shard_map/ppermute | solution.py:285
  10.2 19.2 %copy-start.16 = (bf16[256,640]{1,0:T(8,128)(2,1)S(1)}, bf16[256,640]{1,0:T(8,128)(2,1)}, u32[]{:S(2)}) copy-start(bf16[256,640]{1,0:T(8,128)(2,1)} %get-tuple-element.60) | copy-start | bytes 983044
  13.2 24.0 %all-to-all-start = ((bf16[32,16,640]{2,1,0:T(8,128)(2,1)}), bf16[32,16,640]{2,1,0:T(8,128)(2,1)S(1)}, u32[]{:S(2)}, u32[]{:S(2)}) async-start(bf16[32,16,640]{2,1,0:T(8,128)(2,1)} %shard_map.130), calls=%async_computation | async-start | bytes 1310720 | tf_op jit(solution)/shard_map/all_to_all | solution.py:685
  19.2 21.7 %collective-permute-start.2 = (bf16[256,640]{1,0:T(8,128)(2,1)}, bf16[256,640]{1,0:T(8,128)(2,1)S(1)}, u32[]{:S(2)}, u32[]{:S(2)}) collective-permute-start(bf16[256,640]{1,0:T(8,128)(2,1)} %get-tuple-element.56), channel_id=1, source_target_pairs={{0,2},{1,3},{2,0},{3,1},{4,6},{5,7},{6,4},{7,5},{8,10},{9,11},{10,... | collective-permute-start | bytes 983048 | tf_op jit(solution)/shard_map/ppermute | solution.py:285
  21.0 19.8 %collective-permute-start.3 = (bf16[256,640]{1,0:T(8,128)(2,1)}, bf16[256,640]{1,0:T(8,128)(2,1)S(1)}, u32[]{:S(2)}, u32[]{:S(2)}) collective-permute-start(bf16[256,640]{1,0:T(8,128)(2,1)} %get-tuple-element.57), channel_id=1, source_target_pairs={{0,4},{1,5},{2,6},{3,7},{4,0},{5,1},{6,2},{7,3},{8,12},{9,13},{10,... | collective-permute-start | bytes 983048 | tf_op jit(solution)/shard_map/ppermute | solution.py:285
  22.5 23.2 %collective-permute-start.4 = (bf16[256,640]{1,0:T(8,128)(2,1)}, bf16[256,640]{1,0:T(8,128)(2,1)S(1)}, u32[]{:S(2)}, u32[]{:S(2)}) collective-permute-start(bf16[256,640]{1,0:T(8,128)(2,1)} %get-tuple-element.58), channel_id=1, source_target_pairs={{0,3},{1,2},{2,1},{3,0},{4,7},{5,6},{6,5},{7,4},{8,11},{9,10},{10,... | collective-permute-start | bytes 983048 | tf_op jit(solution)/shard_map/ppermute | solution.py:285
  22.5 8.4 %copy-start.4 = (bf16[256,640]{1,0:T(8,128)(2,1)}, bf16[256,640]{1,0:T(8,128)(2,1)S(1)}, u32[]{:S(2)}) copy-start(bf16[256,640]{1,0:T(8,128)(2,1)S(1)} %collective-permute-done.refs_2_.refs_5_.refs_11_) | copy-start | bytes 983044
  22.5 23.6 %collective-permute-start.5 = (bf16[256,640]{1,0:T(8,128)(2,1)}, bf16[256,640]{1,0:T(8,128)(2,1)S(1)}, u32[]{:S(2)}, u32[]{:S(2)}) collective-permute-start(bf16[256,640]{1,0:T(8,128)(2,1)} %get-tuple-element.59), channel_id=1, source_target_pairs={{0,5},{1,4},{2,7},{3,6},{4,1},{5,0},{6,3},{7,2},{8,13},{9,12},{10,... | collective-permute-start | bytes 983048 | tf_op jit(solution)/shard_map/ppermute | solution.py:285
  29.4 1.5 copy-start.5
  29.4 1.5 copy-start.14
  29.4 16.8 %collective-permute-start.6 = (bf16[256,640]{1,0:T(8,128)(2,1)S(1)}, bf16[256,640]{1,0:T(8,128)(2,1)S(1)}, u32[]{:S(2)}, u32[]{:S(2)}) collective-permute-start(bf16[256,640]{1,0:T(8,128)(2,1)S(1)} %copy-done.16), channel_id=1, source_target_pairs={{0,1},{1,0},{2,3},{3,2},{4,5},{5,4},{6,7},{7,6},{8,9},{9,8},{10,11... | collective-permute-start | bytes 983048 | tf_op jit(solution)/shard_map/ppermute | solution.py:285
  37.2 0.8 copy-start.3
  40.9 5.3 %copy-start.6 = (bf16[256,640]{1,0:T(8,128)(2,1)}, bf16[256,640]{1,0:T(8,128)(2,1)S(1)}, u32[]{:S(2)}) copy-start(bf16[256,640]{1,0:T(8,128)(2,1)S(1)} %collective-permute-done.2.refs_4_.refs_7_.refs_13_) | copy-start | bytes 983044
  40.9 5.3 %copy-start.7 = (bf16[256,640]{1,0:T(8,128)(2,1)}, bf16[256,640]{1,0:T(8,128)(2,1)S(1)}, u32[]{:S(2)}) copy-start(bf16[256,640]{1,0:T(8,128)(2,1)S(1)} %collective-permute-done.3.refs_5_.refs_8_.refs_14_) | copy-start | bytes 983044
  45.7 0.7 copy-start.8
  46.2 0.8 copy-start.10
  49.7 18.5 %collective-permute-start.7 = (bf16[2,256,640]{2,1,0:T(8,128)(2,1)}, bf16[2,256,640]{2,1,0:T(8,128)(2,1)S(1)}, u32[]{:S(2)}, u32[]{:S(2)}) collective-permute-start(bf16[2,256,640]{2,1,0:T(8,128)(2,1)} %shard_map.133.refs_12_), channel_id=1, source_target_pairs={{0,8},{1,9},{2,10},{3,11},{4,12},{5,13},{6,14},{7,15},{8,16},{9,17... | collective-permute-start | bytes 1966088 | tf_op jit(solution)/shard_map/ppermute | solution.py:597
  64.3 21.7 %all-to-all-start.1 = ((bf16[32,16,640]{2,1,0:T(8,128)(2,1)}), bf16[32,16,640]{2,1,0:T(8,128)(2,1)S(1)}, u32[]{:S(2)}, u32[]{:S(2)}) async-start(bf16[32,16,640]{2,1,0:T(8,128)(2,1)} %shard_map.134.refs_3_), calls=%async_computation.1 | async-start | bytes 1310720 | tf_op jit(solution)/shard_map/all_to_all | solution.py:685
  68.1 0.9 copy-start.15
  72.6 4.9 %collective-permute-start.8 = (bf16[144,640]{1,0:T(8,128)(2,1)}, bf16[144,640]{1,0:T(8,128)(2,1)S(1)}, u32[]{:S(2)}, u32[]{:S(2)}) collective-permute-start(bf16[144,640]{1,0:T(8,128)(2,1)} %get-tuple-element.61), channel_id=1, source_target_pairs={{0,1},{1,0},{2,3},{3,2},{4,5},{5,4},{6,7},{7,6},{8,9},{9,8},{10,11... | collective-permute-start | bytes 552968 | tf_op jit(solution)/shard_map/ppermute | solution.py:285
  72.9 10.4 %collective-permute-start.9 = (bf16[144,640]{1,0:T(8,128)(2,1)}, bf16[144,640]{1,0:T(8,128)(2,1)S(1)}, u32[]{:S(2)}, u32[]{:S(2)}) collective-permute-start(bf16[144,640]{1,0:T(8,128)(2,1)} %get-tuple-element.62), channel_id=1, source_target_pairs={{0,6},{1,7},{2,4},{3,5},{4,2},{5,3},{6,0},{7,1},{8,14},{9,15},{10,... | collective-permute-start | bytes 552968 | tf_op jit(solution)/shard_map/ppermute | solution.py:285
  75.5 19.6 %collective-permute-start.10 = (bf16[144,640]{1,0:T(8,128)(2,1)}, bf16[144,640]{1,0:T(8,128)(2,1)S(1)}, u32[]{:S(2)}, u32[]{:S(2)}) collective-permute-start(bf16[144,640]{1,0:T(8,128)(2,1)} %get-tuple-element.65), channel_id=1, source_target_pairs={{0,2},{1,3},{2,0},{3,1},{4,6},{5,7},{6,4},{7,5},{8,10},{9,11},{10,... | collective-permute-start | bytes 552968 | tf_op jit(solution)/shard_map/ppermute | solution.py:285
  76.1 19.1 %collective-permute-start.11 = (bf16[144,640]{1,0:T(8,128)(2,1)}, bf16[144,640]{1,0:T(8,128)(2,1)S(1)}, u32[]{:S(2)}, u32[]{:S(2)}) collective-permute-start(bf16[144,640]{1,0:T(8,128)(2,1)} %get-tuple-element.66), channel_id=1, source_target_pairs={{0,3},{1,2},{2,1},{3,0},{4,7},{5,6},{6,5},{7,4},{8,11},{9,10},{10,... | collective-permute-start | bytes 552968 | tf_op jit(solution)/shard_map/ppermute | solution.py:285
  77.0 18.2 %collective-permute-start.12 = (bf16[144,640]{1,0:T(8,128)(2,1)}, bf16[144,640]{1,0:T(8,128)(2,1)S(1)}, u32[]{:S(2)}, u32[]{:S(2)}) collective-permute-start(bf16[144,640]{1,0:T(8,128)(2,1)} %get-tuple-element.67), channel_id=1, source_target_pairs={{0,4},{1,5},{2,6},{3,7},{4,0},{5,1},{6,2},{7,3},{8,12},{9,13},{10,... | collective-permute-start | bytes 552968 | tf_op jit(solution)/shard_map/ppermute | solution.py:285
  77.5 8.5 %copy-start.11 = (bf16[144,640]{1,0:T(8,128)(2,1)}, bf16[144,640]{1,0:T(8,128)(2,1)S(1)}, u32[]{:S(2)}) copy-start(bf16[144,640]{1,0:T(8,128)(2,1)S(1)} %collective-permute-done.8.refs_5_.refs_3_.refs_6_) | copy-start | bytes 552964
  77.5 17.7 %collective-permute-start.13 = (bf16[144,640]{1,0:T(8,128)(2,1)}, bf16[144,640]{1,0:T(8,128)(2,1)S(1)}, u32[]{:S(2)}, u32[]{:S(2)}) collective-permute-start(bf16[144,640]{1,0:T(8,128)(2,1)} %get-tuple-element.68), channel_id=1, source_target_pairs={{0,5},{1,4},{2,7},{3,6},{4,1},{5,0},{6,3},{7,2},{8,13},{9,12},{10,... | collective-permute-start | bytes 552968 | tf_op jit(solution)/shard_map/ppermute | solution.py:285
  83.4 2.7 %copy-start.12 = (bf16[144,640]{1,0:T(8,128)(2,1)}, bf16[144,640]{1,0:T(8,128)(2,1)S(1)}, u32[]{:S(2)}) copy-start(bf16[144,640]{1,0:T(8,128)(2,1)S(1)} %collective-permute-done.9.refs_6_.refs_8_.refs_11_) | copy-start | bytes 552964
  83.4 12.5 %collective-permute-start.14 = (bf16[144,640]{1,0:T(8,128)(2,1)}, bf16[144,640]{1,0:T(8,128)(2,1)S(1)}, u32[]{:S(2)}, u32[]{:S(2)}) collective-permute-start(bf16[144,640]{1,0:T(8,128)(2,1)} %get-tuple-element.69), channel_id=1, source_target_pairs={{0,7},{1,6},{2,5},{3,4},{4,3},{5,2},{6,1},{7,0},{8,15},{9,14},{10,... | collective-permute-start | bytes 552968 | tf_op jit(solution)/shard_map/ppermute | solution.py:285
  86.1 0.8 copy-start.1
  90.5 22.5 %all-to-all-start.2 = ((bf16[32,16,640]{2,1,0:T(8,128)(2,1)}), bf16[32,16,640]{2,1,0:T(8,128)(2,1)S(1)}, u32[]{:S(2)}, u32[]{:S(2)}) async-start(bf16[32,16,640]{2,1,0:T(8,128)(2,1)} %get-tuple-element.63.refs_18_), calls=%async_computation.2 | async-start | bytes 1310720 | tf_op jit(solution)/shard_map/all_to_all | solution.py:685
  95.1 0.8 copy-start.17
  95.2 0.8 copy-start.18
  95.2 0.8 copy-start.19
  95.2 0.8 copy-start.20
  107.9 8.5 %collective-permute-start.15 = (bf16[128,640]{1,0:T(8,128)(2,1)}, bf16[128,640]{1,0:T(8,128)(2,1)S(1)}, u32[]{:S(2)}, u32[]{:S(2)}) collective-permute-start(bf16[128,640]{1,0:T(8,128)(2,1)} %get-tuple-element.76), channel_id=1, source_target_pairs={{0,1},{1,0},{2,3},{3,2},{4,5},{5,4},{6,7},{7,6},{8,9},{9,8},{10,11... | collective-permute-start | bytes 491528 | tf_op jit(solution)/shard_map/ppermute | solution.py:285
  108.0 10.6 %collective-permute-start.16 = (bf16[128,640]{1,0:T(8,128)(2,1)}, bf16[128,640]{1,0:T(8,128)(2,1)S(1)}, u32[]{:S(2)}, u32[]{:S(2)}) collective-permute-start(bf16[128,640]{1,0:T(8,128)(2,1)} %get-tuple-element.77), channel_id=1, source_target_pairs={{0,2},{1,3},{2,0},{3,1},{4,6},{5,7},{6,4},{7,5},{8,10},{9,11},{10,... | collective-permute-start | bytes 491528 | tf_op jit(solution)/shard_map/ppermute | solution.py:285
  109.2 17.7 %collective-permute-start.17 = (bf16[128,640]{1,0:T(8,128)(2,1)}, bf16[128,640]{1,0:T(8,128)(2,1)S(1)}, u32[]{:S(2)}, u32[]{:S(2)}) collective-permute-start(bf16[128,640]{1,0:T(8,128)(2,1)} %get-tuple-element.78), channel_id=1, source_target_pairs={{0,3},{1,2},{2,1},{3,0},{4,7},{5,6},{6,5},{7,4},{8,11},{9,10},{10,... | collective-permute-start | bytes 491528 | tf_op jit(solution)/shard_map/ppermute | solution.py:285
  109.8 18.9 %collective-permute-start.18 = (bf16[128,640]{1,0:T(8,128)(2,1)}, bf16[128,640]{1,0:T(8,128)(2,1)S(1)}, u32[]{:S(2)}, u32[]{:S(2)}) collective-permute-start(bf16[128,640]{1,0:T(8,128)(2,1)} %get-tuple-element.79), channel_id=1, source_target_pairs={{0,4},{1,5},{2,6},{3,7},{4,0},{5,1},{6,2},{7,3},{8,12},{9,13},{10,... | collective-permute-start | bytes 491528 | tf_op jit(solution)/shard_map/ppermute | solution.py:285
  110.9 19.2 %collective-permute-start.19 = (bf16[128,640]{1,0:T(8,128)(2,1)}, bf16[128,640]{1,0:T(8,128)(2,1)S(1)}, u32[]{:S(2)}, u32[]{:S(2)}) collective-permute-start(bf16[128,640]{1,0:T(8,128)(2,1)} %get-tuple-element.80), channel_id=1, source_target_pairs={{0,5},{1,4},{2,7},{3,6},{4,1},{5,0},{6,3},{7,2},{8,13},{9,12},{10,... | collective-permute-start | bytes 491528 | tf_op jit(solution)/shard_map/ppermute | solution.py:285
  113.0 0.8 copy-start.2
  116.3 10.6 %copy-start.22 = (bf16[128,640]{1,0:T(8,128)(2,1)}, bf16[128,640]{1,0:T(8,128)(2,1)S(1)}, u32[]{:S(2)}) copy-start(bf16[128,640]{1,0:T(8,128)(2,1)S(1)} %collective-permute-done.15.refs_13_.refs_11_) | copy-start | bytes 491524
  116.3 13.9 %collective-permute-start.20 = (bf16[128,640]{1,0:T(8,128)(2,1)}, bf16[128,640]{1,0:T(8,128)(2,1)S(1)}, u32[]{:S(2)}, u32[]{:S(2)}) collective-permute-start(bf16[128,640]{1,0:T(8,128)(2,1)} %get-tuple-element.81), channel_id=1, source_target_pairs={{0,6},{1,7},{2,4},{3,5},{4,2},{5,3},{6,0},{7,1},{8,14},{9,15},{10,... | collective-permute-start | bytes 491528 | tf_op jit(solution)/shard_map/ppermute | solution.py:285
  118.6 8.3 %copy-start.23 = (bf16[128,640]{1,0:T(8,128)(2,1)}, bf16[128,640]{1,0:T(8,128)(2,1)S(1)}, u32[]{:S(2)}) copy-start(bf16[128,640]{1,0:T(8,128)(2,1)S(1)} %collective-permute-done.16.refs_14_.refs_12_) | copy-start | bytes 491524
  118.6 12.8 %collective-permute-start.21 = (bf16[128,640]{1,0:T(8,128)(2,1)}, bf16[128,640]{1,0:T(8,128)(2,1)S(1)}, u32[]{:S(2)}, u32[]{:S(2)}) collective-permute-start(bf16[128,640]{1,0:T(8,128)(2,1)} %get-tuple-element.82), channel_id=1, source_target_pairs={{0,7},{1,6},{2,5},{3,4},{4,3},{5,2},{6,1},{7,0},{8,15},{9,14},{10,... | collective-permute-start | bytes 491528 | tf_op jit(solution)/shard_map/ppermute | solution.py:285
  126.9 6.1 %copy-start.24 = (bf16[128,640]{1,0:T(8,128)(2,1)}, bf16[128,640]{1,0:T(8,128)(2,1)S(1)}, u32[]{:S(2)}) copy-start(bf16[128,640]{1,0:T(8,128)(2,1)S(1)} %collective-permute-done.17.refs_15_.refs_13_) | copy-start | bytes 491524
  126.9 20.2 %collective-permute-start.22 = (bf16[128,640]{1,0:T(8,128)(2,1)}, bf16[128,640]{1,0:T(8,128)(2,1)S(1)}, u32[]{:S(2)}, u32[]{:S(2)}) collective-permute-start(bf16[128,640]{1,0:T(8,128)(2,1)} %get-tuple-element.83), channel_id=1, source_target_pairs={{0,3},{1,2},{2,1},{3,0},{4,7},{5,6},{6,5},{7,4},{8,11},{9,10},{10,... | collective-permute-start | bytes 491528 | tf_op jit(solution)/shard_map/ppermute | solution.py:285
  128.6 4.4 %copy-start.25 = (bf16[128,640]{1,0:T(8,128)(2,1)}, bf16[128,640]{1,0:T(8,128)(2,1)S(1)}, u32[]{:S(2)}) copy-start(bf16[128,640]{1,0:T(8,128)(2,1)S(1)} %collective-permute-done.18.refs_16_.refs_14_) | copy-start | bytes 491524
  128.7 18.5 %collective-permute-start.23 = (bf16[128,640]{1,0:T(8,128)(2,1)}, bf16[128,640]{1,0:T(8,128)(2,1)S(1)}, u32[]{:S(2)}, u32[]{:S(2)}) collective-permute-start(bf16[128,640]{1,0:T(8,128)(2,1)} %get-tuple-element.84), channel_id=1, source_target_pairs={{0,4},{1,5},{2,6},{3,7},{4,0},{5,1},{6,2},{7,3},{8,12},{9,13},{10,... | collective-permute-start | bytes 491528 | tf_op jit(solution)/shard_map/ppermute | solution.py:285
  130.1 2.9 %copy-start.26 = (bf16[128,640]{1,0:T(8,128)(2,1)}, bf16[128,640]{1,0:T(8,128)(2,1)S(1)}, u32[]{:S(2)}) copy-start(bf16[128,640]{1,0:T(8,128)(2,1)S(1)} %collective-permute-done.19.refs_17_.refs_15_) | copy-start | bytes 491524
  130.1 17.1 %collective-permute-start.24 = (bf16[128,640]{1,0:T(8,128)(2,1)}, bf16[128,640]{1,0:T(8,128)(2,1)S(1)}, u32[]{:S(2)}, u32[]{:S(2)}) collective-permute-start(bf16[128,640]{1,0:T(8,128)(2,1)} %get-tuple-element.85), channel_id=1, source_target_pairs={{0,5},{1,4},{2,7},{3,6},{4,1},{5,0},{6,3},{7,2},{8,13},{9,12},{10,... | collective-permute-start | bytes 491528 | tf_op jit(solution)/shard_map/ppermute | solution.py:285
  130.2 2.9 %copy-start.27 = (bf16[128,640]{1,0:T(8,128)(2,1)}, bf16[128,640]{1,0:T(8,128)(2,1)S(1)}, u32[]{:S(2)}) copy-start(bf16[128,640]{1,0:T(8,128)(2,1)S(1)} %collective-permute-done.20.refs_18_.refs_16_) | copy-start | bytes 491524
  130.2 17.0 %collective-permute-start.25 = (bf16[128,640]{1,0:T(8,128)(2,1)}, bf16[128,640]{1,0:T(8,128)(2,1)S(1)}, u32[]{:S(2)}, u32[]{:S(2)}) collective-permute-start(bf16[128,640]{1,0:T(8,128)(2,1)} %get-tuple-element.86), channel_id=1, source_target_pairs={{0,6},{1,7},{2,4},{3,5},{4,2},{5,3},{6,0},{7,1},{8,14},{9,15},{10,... | collective-permute-start | bytes 491528 | tf_op jit(solution)/shard_map/ppermute | solution.py:285
  131.4 1.6 copy-start.28
  131.4 15.8 %collective-permute-start.26 = (bf16[128,640]{1,0:T(8,128)(2,1)}, bf16[128,640]{1,0:T(8,128)(2,1)S(1)}, u32[]{:S(2)}, u32[]{:S(2)}) collective-permute-start(bf16[128,640]{1,0:T(8,128)(2,1)} %get-tuple-element.87), channel_id=1, source_target_pairs={{0,7},{1,6},{2,5},{3,4},{4,3},{5,2},{6,1},{7,0},{8,15},{9,14},{10,... | collective-permute-start | bytes 491528 | tf_op jit(solution)/shard_map/ppermute | solution.py:285
  137.8 27.6 %all-to-all-start.3 = ((bf16[32,16,640]{2,1,0:T(8,128)(2,1)}), bf16[32,16,640]{2,1,0:T(8,128)(2,1)S(1)}, u32[]{:S(2)}, u32[]{:S(2)}) async-start(bf16[32,16,640]{2,1,0:T(8,128)(2,1)} %shard_map.140.refs_3_), calls=%async_computation.3 | async-start | bytes 1310720 | tf_op jit(solution)/shard_map/all_to_all | solution.py:685
  147.2 0.8 copy-start.31
  147.2 0.8 copy-start.32
  147.3 0.8 copy-start.33
  148.1 4.5 %copy-start.13 = (f32[2560]{0:T(1024)S(1)}, f32[2560]{0:T(1024)}, u32[]{:S(2)}) copy-start(f32[2560]{0:T(1024)} %param.19) | copy-start | bytes 30724
  150.6 2.8 %collective-permute-start.27 = (bf16[128,640]{1,0:T(8,128)(2,1)}, bf16[128,640]{1,0:T(8,128)(2,1)S(1)}, u32[]{:S(2)}, u32[]{:S(2)}) collective-permute-start(bf16[128,640]{1,0:T(8,128)(2,1)} %get-tuple-element.88.refs_18_), channel_id=1, source_target_pairs={{0,1},{1,0},{2,3},{3,2},{4,5},{5,4},{6,7},{7,6},{8,9},{9,8},{10,11... | collective-permute-start | bytes 491528 | tf_op jit(solution)/shard_map/ppermute | solution.py:285
  150.9 9.4 %collective-permute-start.28 = (bf16[128,640]{1,0:T(8,128)(2,1)}, bf16[128,640]{1,0:T(8,128)(2,1)S(1)}, u32[]{:S(2)}, u32[]{:S(2)}) collective-permute-start(bf16[128,640]{1,0:T(8,128)(2,1)} %get-tuple-element.89), channel_id=1, source_target_pairs={{0,2},{1,3},{2,0},{3,1},{4,6},{5,7},{6,4},{7,5},{8,10},{9,11},{10,... | collective-permute-start | bytes 491528 | tf_op jit(solution)/shard_map/ppermute | solution.py:285
  153.4 6.9 %copy-start.34 = (bf16[128,640]{1,0:T(8,128)(2,1)}, bf16[128,640]{1,0:T(8,128)(2,1)S(1)}, u32[]{:S(2)}) copy-start(bf16[128,640]{1,0:T(8,128)(2,1)S(1)} %collective-permute-done.27.refs_3_) | copy-start | bytes 491524
  165.5 0.9 copy-start
  (5 other events, 3.5 us)
